TPU v7x, 256 devices: a whole 4x4x8 slice. The times are simulated.
256 devices in a mesh: dom: 16 (over y, x), freq: 16 (over z, core).
Axes of the slice: x: 4, y: 4, z: 8, core: 2. Of those that a mesh axis runs over, the one named last changes fastest.
Arguments:
- voltages: float32 [512, 32768], P('freq', 'dom'), may hold values from -5 to 5
- sources: float32 [512, 32768], P('freq', 'dom'), may hold values from -20 to 20
- terminals: int32 [2, 65536], P(None, 'dom'), may hold values from 0 to 4095, as said below
- elem_current: float32 [2, 65536], P(None, 'dom'), may hold values from 0.2 to 2
- elem_charge: float32 [2, 65536], P(None, 'dom'), may hold values from 0.1 to 1
- jacobi: float32 [256, 2, 2, 32768], P('freq', None, None, 'dom'), may hold values from -1.2 to 2
Outputs:
- residual: float32 [512, 32768], P('freq', 'dom')
- newton_step: float32 [512, 32768], P('freq', 'dom')
- residual_norm: float32 [], replicated
Inputs may be any that keep to these rules, and one draw needn't show every extreme that they name: `terminals`: A terminal value below 2048 is a node of the element's own partition; a value v of 2048 or more is node (v - 2048) % 128 of partition (v - 2048) // 128, one of that partition's first 128 nodes.
All inputs are finite; a program needn't handle non-finite values.
Results may differ from a plain program's by a relative error of at most 0.0003.
Values sent between devices are 32-bit elements; how exact they have to be, the bound alone decides.
No kernel may reach another device: no remote copies, remote signals or barrier semaphores. Data moves between devices by JAX's collectives and lax.ppermute only.
A program may use at most 64 MiB of HBM per device.

v0:
```python
import math

import jax
import jax.numpy as jnp
from jax import lax
from jax.sharding import PartitionSpec as P

S = 512


trust_radius = 2.0


def transform_table(samples):
    row_index = jnp.arange(samples, dtype=jnp.int32)
    harmonic = row_index // 2
    is_sine = row_index % 2 == 1
    column = jnp.arange(samples, dtype=jnp.int32)
    order = jnp.where(harmonic == 0, jnp.where(is_sine, samples // 2, 0), harmonic)
    phase = (order[:, None] * column[None, :] % samples).astype(jnp.float32) * (
        2.0 * math.pi / samples
    )
    use_sine = is_sine & (harmonic > 0)
    values = jnp.where(use_sine[:, None], jnp.sin(phase), jnp.cos(phase))
    weight = jnp.where(harmonic == 0, math.sqrt(1.0 / samples), math.sqrt(2.0 / samples)).astype(
        jnp.float32
    )
    forward = values * weight[:, None]
    pairs = forward.reshape(samples // 2, 2, samples)
    rate = 2.0 / samples * jnp.arange(samples // 2, dtype=jnp.float32)
    derived = jnp.stack([pairs[:, 1], -pairs[:, 0]], axis=1) * rate[:, None, None]
    return jnp.concatenate([forward, derived.reshape(samples, samples)], axis=1)


def incidence_sum(flows, terminals, column_count):
    flow_rows = flows.shape[0]
    elem_count = flows.shape[1]
    block_size = math.gcd(elem_count, 512)
    block_count = elem_count // block_size
    flow_blocks = flows.reshape(flow_rows, block_count, block_size).transpose(1, 0, 2)
    term_blocks = terminals.reshape(2, block_count, block_size).transpose(1, 0, 2)
    columns = jnp.arange(column_count, dtype=jnp.int32)

    def accumulate(total, pieces):
        flow_piece, term_piece = pieces
        plus = (term_piece[0][:, None] == columns[None, :]).astype(jnp.float32)
        minus = (term_piece[1][:, None] == columns[None, :]).astype(jnp.float32)
        signed = plus - minus
        total = total + jnp.dot(
            flow_piece, signed, precision=lax.Precision.HIGHEST, preferred_element_type=jnp.float32
        )
        return (total, None)

    start = jnp.zeros((flow_rows, column_count), jnp.float32)
    total, unused = lax.scan(accumulate, start, (flow_blocks, term_blocks))
    return total


def body(voltages, sources, terminals, elem_current, elem_charge, jacobi):
    sample_rows, node_count = voltages.shape
    border_count = node_count // 16
    border = lax.all_gather(voltages[:, :border_count], "dom", axis=1, tiled=True)
    extended = jnp.concatenate([voltages, border], axis=1)
    across = extended[:, terminals[0]] - extended[:, terminals[1]]
    current = elem_current[0][None, :] * across + elem_current[1][None, :] * jnp.tanh(2.0 * across)
    charge = elem_charge[0][None, :] * across + elem_charge[1][None, :] * jnp.tanh(across)
    flows = jnp.concatenate([current, charge], axis=0)
    totals = incidence_sum(flows, terminals, extended.shape[1]).reshape(
        2, sample_rows, extended.shape[1]
    )
    incoming = lax.psum_scatter(totals[:, :, node_count:], "dom", scatter_dimension=2, tiled=True)
    owned = totals[:, :, :node_count]
    owned = jnp.concatenate(
        [owned[:, :, :border_count] + incoming, owned[:, :, border_count:]], axis=2
    )
    table = transform_table(S)
    first_sample = lax.axis_index("freq") * sample_rows
    direct = lax.dynamic_slice_in_dim(table, first_sample, sample_rows, 1)
    slope = lax.dynamic_slice_in_dim(table, S + first_sample, sample_rows, 1)
    columns = jnp.concatenate([direct, slope], axis=1)
    stacked = owned.reshape(2 * sample_rows, node_count)
    transformed = lax.psum_scatter(
        jnp.dot(
            columns, stacked, precision=lax.Precision.HIGHEST, preferred_element_type=jnp.float32
        ),
        "freq",
        scatter_dimension=0,
        tiled=True,
    )
    residual = transformed - sources
    pairs = residual.reshape(sample_rows // 2, 2, node_count)
    raw = -(jacobi[:, :, 0, :] * pairs[:, 0:1, :] + jacobi[:, :, 1, :] * pairs[:, 1:2, :])
    raw = raw.reshape(sample_rows, node_count)
    step_squares, residual_squares = lax.psum(
        (jnp.sum(raw * raw), jnp.sum(residual * residual)), ("dom", "freq")
    )
    entry_count = S * node_count * lax.axis_size("dom")
    spread = jnp.sqrt(step_squares / entry_count + 1e-06)
    newton_step = raw * jnp.minimum(1.0, trust_radius / spread)
    residual_norm = jnp.sqrt(residual_squares)
    return (residual, newton_step, residual_norm)


def solution(mesh):
    placed = (
        P("freq", "dom"),
        P("freq", "dom"),
        P(None, "dom"),
        P(None, "dom"),
        P(None, "dom"),
        P("freq", None, None, "dom"),
    )
    return jax.shard_map(
        body,
        mesh=mesh,
        in_specs=placed,
        out_specs=(P("freq", "dom"), P("freq", "dom"), P()),
        check_vma=False,
    )
```

profile of v0, /device:TPU:1, one launch (start us, length us, event | category | flops | bytes accessed | tf_op | source)
XLA Modules:
  0.0 364.6 jit_solution(12035438453833443217)
XLA Ops:
  8.0 19.6 %all_gather.3 = f32[32,2048]{1,0:T(8,128)S(1)} all-gather(f32[32,128]{1,0:T(8,128)S(1)} %slice.62), channel_id=1, replica_groups=mesh['dom'=16,'freq'=16] {'dom'}, dimensions={1}, use_global_device_ids=true | all-gather | bytes 278528 | tf_op jit(solution)/shard_map/all_gather | solution.py:62
  27.5 1.0 pad_maximum_fusion.1
  29.2 14.1 %gather_fusion = f32[4096,32]{1,0:T(8,128)} fusion(f32[32,4096]{0,1:T(8,128)S(1)} %copy.21, s32[4096]{0:T(1024)S(1)} %broadcast_clamp_fusion.1), kind=kCustom, calls=%fused_computation | custom fusion | bytes 1064960 | tf_op jit(solution)/shard_map/gather | solution.py:64
  43.3 14.1 %gather_fusion.1 = f32[4096,32]{1,0:T(8,128)} fusion(f32[32,4096]{0,1:T(8,128)S(1)} %copy.21, s32[4096]{0:T(1024)S(1)} %broadcast_clamp_fusion), kind=kCustom, calls=%fused_computation.1 | custom fusion | bytes 1064960 | tf_op jit(solution)/shard_map/gather | solution.py:64
  57.4 2.4 sub.30
  61.8 57.4 %while.12 = (s32[]{:T(128)}, f32[64,4096]{1,0:T(8,128)S(1)}, f32[8,64,512]{2,1,0:T(8,128)S(1)}, s32[8,2,512]{2,1,0:T(2,128)S(1)}, s32[]{:T(128)}, /*index=5*/s32[]{:T(128)}, s32[]{}) while((s32[]{:T(128)}, f32[64,4096]{1,0:T(8,128)S(1)}, f32[8,64,512]{2,1,0:T(8,128)S(1)}, s32[8,2,512]{2,1,0:T(2,128)S(1)}, s32[]{:T(128)}, ...), condition=%wide.region_1.2_spmd.clone.clone, body=%wide.region_0.1_spmd.clone.clone.sunk | while | flops 1621622784 | bytes 2240623 | solution.py:55
  61.8 7.1 %fusion.56 = f32[64,4096]{1,0:T(8,128)S(1)} fusion(s32[512]{0:T(512)S(1)} %bitcast.47, s32[512]{0:T(512)S(1)} %bitcast.46, f32[64,4096]{1,0:T(8,128)S(1)} %get-tuple-element.135, pred[]{:T(512)S(6)} %compare.14, f32[8,64,512]{2,1,0:T(8,128)S(1)} %get-tuple-element.143, s32[]{:T(128)} %get-tuple-element.134), kind=kOutput, calls=%fused_computation.9.clone.1 | convolution fusion | flops 1621622784 | bytes 2232325 | tf_op jit(solution)/shard_map/while/body/eval_jaxpr/dot_general | solution.py:49
  69.0 7.1 %fusion.56 = f32[64,4096]{1,0:T(8,128)S(1)} fusion(s32[512]{0:T(512)S(1)} %bitcast.47, s32[512]{0:T(512)S(1)} %bitcast.46, f32[64,4096]{1,0:T(8,128)S(1)} %get-tuple-element.135, pred[]{:T(512)S(6)} %compare.14, f32[8,64,512]{2,1,0:T(8,128)S(1)} %get-tuple-element.143, s32[]{:T(128)} %get-tuple-element.134), kind=kOutput, calls=%fused_computation.9.clone.1 | convolution fusion | flops 1621622784 | bytes 2232325 | tf_op jit(solution)/shard_map/while/body/eval_jaxpr/dot_general | solution.py:49
  76.2 7.1 %fusion.56 = f32[64,4096]{1,0:T(8,128)S(1)} fusion(s32[512]{0:T(512)S(1)} %bitcast.47, s32[512]{0:T(512)S(1)} %bitcast.46, f32[64,4096]{1,0:T(8,128)S(1)} %get-tuple-element.135, pred[]{:T(512)S(6)} %compare.14, f32[8,64,512]{2,1,0:T(8,128)S(1)} %get-tuple-element.143, s32[]{:T(128)} %get-tuple-element.134), kind=kOutput, calls=%fused_computation.9.clone.1 | convolution fusion | flops 1621622784 | bytes 2232325 | tf_op jit(solution)/shard_map/while/body/eval_jaxpr/dot_general | solution.py:49
  83.4 7.1 %fusion.56 = f32[64,4096]{1,0:T(8,128)S(1)} fusion(s32[512]{0:T(512)S(1)} %bitcast.47, s32[512]{0:T(512)S(1)} %bitcast.46, f32[64,4096]{1,0:T(8,128)S(1)} %get-tuple-element.135, pred[]{:T(512)S(6)} %compare.14, f32[8,64,512]{2,1,0:T(8,128)S(1)} %get-tuple-element.143, s32[]{:T(128)} %get-tuple-element.134), kind=kOutput, calls=%fused_computation.9.clone.1 | convolution fusion | flops 1621622784 | bytes 2232325 | tf_op jit(solution)/shard_map/while/body/eval_jaxpr/dot_general | solution.py:49
  90.6 7.1 %fusion.56 = f32[64,4096]{1,0:T(8,128)S(1)} fusion(s32[512]{0:T(512)S(1)} %bitcast.47, s32[512]{0:T(512)S(1)} %bitcast.46, f32[64,4096]{1,0:T(8,128)S(1)} %get-tuple-element.135, pred[]{:T(512)S(6)} %compare.14, f32[8,64,512]{2,1,0:T(8,128)S(1)} %get-tuple-element.143, s32[]{:T(128)} %get-tuple-element.134), kind=kOutput, calls=%fused_computation.9.clone.1 | convolution fusion | flops 1621622784 | bytes 2232325 | tf_op jit(solution)/shard_map/while/body/eval_jaxpr/dot_general | solution.py:49
  97.7 7.1 %fusion.56 = f32[64,4096]{1,0:T(8,128)S(1)} fusion(s32[512]{0:T(512)S(1)} %bitcast.47, s32[512]{0:T(512)S(1)} %bitcast.46, f32[64,4096]{1,0:T(8,128)S(1)} %get-tuple-element.135, pred[]{:T(512)S(6)} %compare.14, f32[8,64,512]{2,1,0:T(8,128)S(1)} %get-tuple-element.143, s32[]{:T(128)} %get-tuple-element.134), kind=kOutput, calls=%fused_computation.9.clone.1 | convolution fusion | flops 1621622784 | bytes 2232325 | tf_op jit(solution)/shard_map/while/body/eval_jaxpr/dot_general | solution.py:49
  104.9 7.1 %fusion.56 = f32[64,4096]{1,0:T(8,128)S(1)} fusion(s32[512]{0:T(512)S(1)} %bitcast.47, s32[512]{0:T(512)S(1)} %bitcast.46, f32[64,4096]{1,0:T(8,128)S(1)} %get-tuple-element.135, pred[]{:T(512)S(6)} %compare.14, f32[8,64,512]{2,1,0:T(8,128)S(1)} %get-tuple-element.143, s32[]{:T(128)} %get-tuple-element.134), kind=kOutput, calls=%fused_computation.9.clone.1 | convolution fusion | flops 1621622784 | bytes 2232325 | tf_op jit(solution)/shard_map/while/body/eval_jaxpr/dot_general | solution.py:49
  112.1 7.1 %fusion.56 = f32[64,4096]{1,0:T(8,128)S(1)} fusion(s32[512]{0:T(512)S(1)} %bitcast.47, s32[512]{0:T(512)S(1)} %bitcast.46, f32[64,4096]{1,0:T(8,128)S(1)} %get-tuple-element.135, pred[]{:T(512)S(6)} %compare.14, f32[8,64,512]{2,1,0:T(8,128)S(1)} %get-tuple-element.143, s32[]{:T(128)} %get-tuple-element.134), kind=kOutput, calls=%fused_computation.9.clone.1 | convolution fusion | flops 1621622784 | bytes 2232325 | tf_op jit(solution)/shard_map/while/body/eval_jaxpr/dot_general | solution.py:49
  119.3 0.9 slice.86
  120.8 18.4 %select_multiply_fusion = f32[256,2,512]{2,1,0:T(2,128)S(1)} fusion(pred[256,2]{1,0:T(8,128)(4,1)S(1)} %fusion.36, f32[256,2]{1,0:T(8,128)S(1)} %compare_select_fusion.2, s32[256,2]{1,0:T(8,128)S(1)} %compare_select_fusion.3), kind=kLoop, calls=%fused_computation.35 | loop fusion | flops 4194304 | bytes 1053184 | tf_op jit(solution)/shard_map/mul | solution.py:28
  140.1 0.9 pad_maximum_fusion
  142.0 4.3 %select_multiply_fusion.1 = f32[512,512]{1,0:T(8,128)S(1)} fusion(f32[512]{0:T(512)S(1)} %compare_select_fusion.6, s32[512]{0:T(512)S(1)} %compare_select_fusion.7, pred[512]{0:T(512)(128)(4,1)S(1)} %fusion.44), kind=kLoop, calls=%fused_computation.36 | loop fusion | flops 4194304 | bytes 1053184 | tf_op jit(solution)/shard_map/mul | solution.py:28
  146.8 55.3 %reduce-scatter.3.cloned.1.call-done = f32[2,32,128]{2,1,0:T(8,128)} async-done(((f32[2,32,2048]{2,1,0:T(8,128)}), f32[2,32,128]{2,1,0:T(8,128)}) %reduce-scatter.3.cloned.1.call-update) | async-done | bytes 32784 | tf_op jit(solution)/shard_map/reduce_scatter | solution.py:71
  202.9 5.1 %fusion.25 = f32[512,2048]{1,0:T(8,128)} fusion(f32[64,2048]{1,0:T(8,128)S(1)} %bitcast.35, f32[512,32]{1,0:T(8,128)S(1)} %get-tuple-element.87, f32[512,32]{1,0:T(8,128)S(1)} %get-tuple-element.86), kind=kOutput, calls=%fused_computation.48 | convolution fusion | flops 805339136 | bytes 4849664 | tf_op jit(solution)/shard_map/dot_general | solution.py:83
  208.0 60.9 %reduce-scatter.5.cloned.1.call-done = f32[32,2048]{1,0:T(8,128)} async-done(((f32[512,2048]{1,0:T(8,128)}), f32[32,2048]{1,0:T(8,128)}) %reduce-scatter.5.cloned.1.call-update) | async-done | bytes 262160 | tf_op jit(solution)/shard_map/reduce_scatter | solution.py:82
  269.0 1.6 multiply_reduce_fusion
  271.1 2.4 multiply_reduce_fusion.1
  273.5 80.0 %all-reduce = (f32[]{:T(128)}, f32[]{:T(128)}) all-reduce(f32[]{:T(128)} %get-tuple-element.65, f32[]{:T(128)} %get-tuple-element.82), channel_id=1, replica_groups=mesh['dom'=16,'freq'=16] {'dom','freq'}, use_global_device_ids=true, to_apply=%region_5.6 | all-reduce | flops 2 | bytes 16 | tf_op jit(solution)/shard_map/psum | solution.py:94
  (69 shorter events, 9.3 us)
Async XLA Ops:
  7.2 22.0 %copy-start.5 = (s32[2,4096]{1,0:T(2,128)S(1)}, s32[2,4096]{1,0:T(2,128)}, u32[]{:S(2)}) copy-start(s32[2,4096]{1,0:T(2,128)} %param.10) | copy-start | bytes 98308
  7.2 194.9 %reduce-scatter.3.cloned.1.call-start = ((), (), s32[]{:S(2)}) async-start(), calls=%async_computation.2 | async-start | bytes 557056 | tf_op jit(solution)/shard_map/reduce_scatter | solution.py:71
  59.8 0.8 copy-start.6
  59.8 0.8 copy-start.7
  60.6 1.2 copy-start
  119.2 20.0 %copy-start.1 = (f32[64,4096]{1,0:T(8,128)}, f32[64,4096]{1,0:T(8,128)S(1)}, u32[]{:S(2)}) copy-start(f32[64,4096]{1,0:T(8,128)S(1)} %get-tuple-element.33) | copy-start | bytes 3145732
  120.2 148.8 %reduce-scatter.5.cloned.1.call-start = ((), (), s32[]{:S(2)}) async-start(), calls=%async_computation.3 | async-start | bytes 4456448 | tf_op jit(solution)/shard_map/reduce_scatter | solution.py:82
  208.0 61.0 %copy-start.4 = (f32[32,2048]{1,0:T(8,128)S(1)}, f32[32,2048]{1,0:T(8,128)}, u32[]{:S(2)}) copy-start(f32[32,2048]{1,0:T(8,128)} %param.9) | copy-start | bytes 786436
  208.0 63.0 %copy-start.3 = (f32[16,2,2,2048]{3,2,1,0:T(2,128)S(1)}, f32[16,2,2,2048]{3,2,1,0:T(2,128)}, u32[]{:S(2)}) copy-start(f32[16,2,2,2048]{3,2,1,0:T(2,128)} %param.13) | copy-start | bytes 1572868
  270.6 84.1 %copy-start.2 = (f32[32,2048]{1,0:T(8,128)}, f32[32,2048]{1,0:T(8,128)S(1)}, u32[]{:S(2)}) copy-start(f32[32,2048]{1,0:T(8,128)S(1)} %get-tuple-element.83) | copy-start | bytes 786436
Sparse Core Ops, SparseCore 0:
  120.3 81.7 reduce-scatter.2
  208.2 60.7 reduce-scatter.4
where the time goes:
time: 365 us
  waiting for transfers between devices  116 us (32%)
  blocking collectives  99.6 us (27%)
  matrix products  62.1 us (17%)
  local copies, waits for them, and re-layouts  34.6 us (9%)
  other arithmetic  34.6 us (9%)
  between operations  16.9 us (5%)
    psum x1, blocking collectives, body(): lax.psum((jnp.sum(raw * raw), jnp.sum(residual * residual)), ('dom', 'fre...  80 us
    reduce_scatter x1, waiting for transfers between devices, body(): lax.psum_scatter(jnp.dot(columns, stacked, precision=lax.Precision.HIGHES...  60.9 us
    dot_general x8, matrix products, accumulate(): jnp.dot(flow_piece, signed, precision=lax.Precision.HIGHEST, preferred_el...  57.1 us
    reduce_scatter x1, waiting for transfers between devices, body(): lax.psum_scatter(totals[:, :, node_count:], 'dom', scatter_dimension=2, t...  55.3 us
    gather x2, local copies, waits for them, and re-layouts, body(): across = extended[:, terminals[0]] - extended[:, terminals[1]]  28.2 us
    mul x2, other arithmetic, transform_table(): forward = values * weight[:, None]  22.7 us
    all_gather x1, blocking collectives, body(): lax.all_gather(voltages[:, :border_count], 'dom', axis=1, tiled=True)  19.6 us
  transfers between devices with their start and end apart: 2, of which 2 were waited for; matrix products, arithmetic and copies ran while one was open for 7% of the time, Pallas kernels for 0%

commit v1 on v0

v1 whole, which is shorter than its diff:
```python
import functools
import math

import jax
import jax.numpy as jnp
import ml_dtypes
import numpy as np
from jax import lax
from jax.experimental import pallas as pl
from jax.experimental.pallas import tpu as pltpu
from jax.sharding import PartitionSpec as P

S = 512
ROWS = 32
NPD = 2048
NE = 4096
NB = 128
PARTS = 16
LANES = 128
LOW = 512
HIGHS = 8
TILE = 512

trust_radius = 2.0
BF = jnp.bfloat16
F32 = jnp.float32


def transform_table():
    row = np.arange(S)
    harmonic = row // 2
    sine = (row % 2 == 1) & (harmonic > 0)
    order = np.where(harmonic == 0, np.where(row % 2 == 1, S // 2, 0), harmonic)
    phase = (order[:, None] * np.arange(S)[None, :] % S) * (2.0 * math.pi / S)
    values = np.where(sine[:, None], np.sin(phase), np.cos(phase))
    weight = np.where(harmonic == 0, math.sqrt(1.0 / S), math.sqrt(2.0 / S))
    forward = values * weight[:, None]
    pairs = forward.reshape(S // 2, 2, S)
    rate = 2.0 / S * np.arange(S // 2)
    derived = (np.stack([pairs[:, 1], -pairs[:, 0]], axis=1) * rate[:, None, None]).reshape(S, S)
    both = np.stack([forward.reshape(S, PARTS, ROWS), derived.reshape(S, PARTS, ROWS)], axis=2)
    return both.reshape(S, 2 * S)


def split(x):
    hi = x.astype(BF)
    return hi, (x - hi.astype(F32)).astype(BF)


def element_kernel(volt_ref, border_ref, term_ref, cur_ref, chg_ref, own_ref, out_ref, table_ref, acc_ref):
    per = LOW // LANES
    for a in range(HIGHS):
        if a * LOW < NPD:
            block = volt_ref[:, a * LOW : (a + 1) * LOW]
        else:
            first = a * per - NPD // LANES
            block = jnp.concatenate([border_ref[first + k] for k in range(per)], axis=1)
        hi, lo = split(block)
        table_ref[a * ROWS : (a + 1) * ROWS, :] = hi
        table_ref[(HIGHS + a) * ROWS : (HIGHS + a + 1) * ROWS, :] = lo
    acc_ref[...] = jnp.zeros_like(acc_ref)
    low_iota = lax.broadcasted_iota(jnp.int32, (LOW, TILE), 0)
    table = table_ref[...]

    def step(i, carry):
        cols = pl.ds(pl.multiple_of(i * TILE, TILE), TILE)
        highs, hots, ends = [], [], []
        for t in range(2):
            node = term_ref[t : t + 1, cols]
            high, low = node >> 9, node & (LOW - 1)
            hot = jnp.where(low_iota == low, 1.0, 0.0).astype(BF)
            found = jnp.dot(table, hot, preferred_element_type=F32)
            value = jnp.zeros((ROWS, TILE), F32)
            for a in range(HIGHS):
                part = found[a * ROWS : (a + 1) * ROWS] + found[(HIGHS + a) * ROWS : (HIGHS + a + 1) * ROWS]
                value = jnp.where(high == a, part, value)
            highs.append(high)
            hots.append(hot)
            ends.append(value)
        across = ends[0] - ends[1]
        current = cur_ref[0:1, cols] * across + cur_ref[1:2, cols] * jnp.tanh(2.0 * across)
        charge = chg_ref[0:1, cols] * across + chg_ref[1:2, cols] * jnp.tanh(across)
        hi, lo = split(jnp.concatenate([current, charge], axis=0))
        flows = jnp.concatenate([hi, lo], axis=0)
        sides = []
        for t in range(2):
            signed = flows if t == 0 else -flows
            sides.append(
                jnp.concatenate(
                    [signed * jnp.where(highs[t] == a, 1.0, 0.0).astype(BF) for a in range(HIGHS)],
                    axis=0,
                )
            )
        acc_ref[...] += lax.dot_general(
            jnp.concatenate(sides, axis=1),
            jnp.concatenate(hots, axis=1),
            (((1,), (1,)), ((), ())),
            preferred_element_type=F32,
        )
        return carry

    lax.fori_loop(0, NE // TILE, step, 0)
    for a in range(HIGHS):
        base = a * 4 * ROWS
        total = acc_ref[base : base + 2 * ROWS, :] + acc_ref[base + 2 * ROWS : base + 4 * ROWS, :]
        for k in range(per):
            block = a * per + k
            piece = total[:, k * LANES : (k + 1) * LANES]
            if block < PARTS:
                own_ref[block] = piece
            else:
                out_ref[block - PARTS] = piece


def transform_kernel(flow_ref, high_ref, low_ref, out_ref):
    hi, lo = split(flow_ref[...])
    dot = functools.partial(jnp.dot, preferred_element_type=F32)
    out_ref[...] = dot(high_ref[...], hi) + (dot(high_ref[...], lo) + dot(low_ref[...], hi))


def step_kernel(coef_ref, src_ref, jac_ref, res_ref, raw_ref, sums_ref):
    even = lax.broadcasted_iota(jnp.int32, (ROWS, LANES), 0) % 2 == 0
    raw_sum = jnp.zeros((ROWS, LANES), F32)
    res_sum = jnp.zeros((ROWS, LANES), F32)
    for k in range(NPD // LANES):
        cols = slice(k * LANES, (k + 1) * LANES)
        res = coef_ref[k] - src_ref[:, cols]
        res_ref[:, cols] = res
        first = jnp.where(even, res, pltpu.roll(res, 1, 0))
        second = jnp.where(even, pltpu.roll(res, ROWS - 1, 0), res)
        raw = -(jac_ref[:, 0, cols] * first + jac_ref[:, 1, cols] * second)
        raw_ref[:, cols] = raw
        raw_sum += raw * raw
        res_sum += res * res
    raw_row = jnp.sum(raw_sum, axis=0, keepdims=True)
    res_row = jnp.sum(res_sum, axis=0, keepdims=True)
    half = lax.broadcasted_iota(jnp.int32, (1, LANES), 1) < LANES // 2
    row = jnp.where(half, raw_row + pltpu.roll(raw_row, LANES // 2, 1), res_row + pltpu.roll(res_row, LANES // 2, 1))
    sums_ref[...] = jnp.broadcast_to(row, sums_ref.shape)


def scale_kernel(raw_ref, sums_ref, out_ref, norm_ref):
    row = jnp.sum(sums_ref[...], axis=0, keepdims=True)
    half = lax.broadcasted_iota(jnp.int32, (1, LANES), 1) < LANES // 2
    raw_sum = jnp.sum(jnp.where(half, row, 0.0), axis=1, keepdims=True)
    res_sum = jnp.sum(jnp.where(half, 0.0, row), axis=1, keepdims=True)
    spread = jnp.sqrt(raw_sum / (S * NPD * PARTS) + 1e-06)
    out_ref[...] = raw_ref[...] * jnp.minimum(1.0, trust_radius / spread)
    norm_ref[...] = jnp.sqrt(res_sum)


def call(kernel, out_shapes, scratch=(), limit=None):
    return pl.pallas_call(
        kernel,
        out_shape=[jax.ShapeDtypeStruct(s, F32) for s in out_shapes],
        scratch_shapes=list(scratch),
        compiler_params=pltpu.CompilerParams(vmem_limit_bytes=limit),
    )


def body(voltages, sources, terminals, elem_current, elem_charge, jacobi):
    sent = jnp.broadcast_to(voltages[None, :, :NB], (PARTS, ROWS, NB))
    border = lax.all_to_all(sent, "dom", 0, 0, tiled=True)
    own, outgoing = call(
        element_kernel,
        [(PARTS, 2 * ROWS, LANES), (PARTS, 2 * ROWS, LANES)],
        [pltpu.VMEM((2 * HIGHS * ROWS, LOW), BF), pltpu.VMEM((HIGHS * 4 * ROWS, LOW), F32)],
        40 * 2**20,
    )(voltages, border, terminals, elem_current, elem_charge)
    incoming = lax.all_to_all(outgoing, "dom", 0, 0, tiled=True)
    own = own.at[0].add(jnp.sum(incoming, axis=0))
    flows = lax.all_to_all(own, "freq", 0, 0, tiled=True).reshape(2 * S, LANES)
    table = transform_table()
    high = table.astype(ml_dtypes.bfloat16)
    low = (table - high.astype(np.float64)).astype(ml_dtypes.bfloat16)
    (coef,) = call(transform_kernel, [(S, LANES)], (), 24 * 2**20)(flows, jnp.asarray(high), jnp.asarray(low))
    coef = lax.all_to_all(coef.reshape(PARTS, ROWS, LANES), "freq", 0, 0, tiled=True)
    residual, raw, sums = call(step_kernel, [(ROWS, NPD), (ROWS, NPD), (256, LANES)], (), 24 * 2**20)(
        coef, sources, jacobi.reshape(ROWS, 2, NPD)
    )
    sums = lax.all_to_all(sums, ("dom", "freq"), 0, 0, tiled=True)
    newton_step, norm = call(scale_kernel, [(ROWS, NPD), (1, 1)], (), 24 * 2**20)(raw, sums)
    return residual, newton_step, norm.reshape(())


def solution(mesh):
    placed = (
        P("freq", "dom"),
        P("freq", "dom"),
        P(None, "dom"),
        P(None, "dom"),
        P(None, "dom"),
        P("freq", None, None, "dom"),
    )
    return jax.shard_map(
        body,
        mesh=mesh,
        in_specs=placed,
        out_specs=(P("freq", "dom"), P("freq", "dom"), P()),
        check_vma=False,
    )
```

time: 365 us -> 110 us (0.30)
  waiting for transfers between devices: 116 us -> 0 us
  matrix products: 62.1 us -> 0 us
  other arithmetic: 34.6 us -> 0.04 us
  local copies, waits for them, and re-layouts: 34.6 us -> 0.78 us
  Pallas kernels: 0 us -> 19.9 us
  between operations: 16.9 us -> 0.73 us
  blocking collectives: 99.6 us -> 88.2 us
    reduce_scatter x2 -> x0, waiting for transfers between devices: 116 us -> none  [the longest x1 60.9 us: body(): lax.psum_scatter(jnp.dot(columns, stacked, precision=lax.Precision.HIGHES...]
    all_to_all x0 -> x5, blocking collectives: none -> 88.2 us  [the longest x1 28.7 us: body(): flows = lax.all_to_all(own, 'freq', 0, 0, tiled=True).reshape(2 * S, LANES)]
    psum x1 -> x0, blocking collectives: 80 us -> none  [body(): lax.psum((jnp.sum(raw * raw), jnp.sum(residual * residual)), ('dom', 'fre...]
    dot_general x9 -> x0, matrix products: 62.1 us -> none  [the longest x8 57.1 us: accumulate(): jnp.dot(flow_piece, signed, precision=lax.Precision.HIGHEST, preferred_el...]
    gather x2 -> x0, local copies, waits for them, and re-layouts: 28.2 us -> none  [body(): across = extended[:, terminals[0]] - extended[:, terminals[1]]]
    mul x5 -> x0, other arithmetic: 23.6 us -> none  [the longest x2 22.7 us: transform_table(): forward = values * weight[:, None]]
    pallas_call x0 -> x4, Pallas kernels: none -> 19.9 us  [the longest x1 16.8 us: body(): call(element_kernel, [(PARTS, 2 * ROWS, LANES), (PARTS, 2 * ROWS, LANES)]...]
    all_gather x1 -> x0, blocking collectives: 19.6 us -> none  [body(): lax.all_gather(voltages[:, :border_count], 'dom', axis=1, tiled=True)]
  transfers between devices with their start and end apart: 2 -> 0, of which waited for: 2 -> 0; matrix products, arithmetic and copies ran while one was open for 7% -> 0% of each run, Pallas kernels for 0% -> 0%
where the time goes in v1:
time: 110 us
  blocking collectives  88.2 us (80%)
  Pallas kernels  19.9 us (18%)
    all_to_all x1, blocking collectives, body(): flows = lax.all_to_all(own, 'freq', 0, 0, tiled=True).reshape(2 * S, LANES)  28.7 us
    all_to_all x1, blocking collectives, body(): sums = lax.all_to_all(sums, ('dom', 'freq'), 0, 0, tiled=True)  17.3 us
    pallas_call x1, Pallas kernels, body(): call(element_kernel, [(PARTS, 2 * ROWS, LANES), (PARTS, 2 * ROWS, LANES)]...  16.8 us
    all_to_all x1, blocking collectives, body(): border = lax.all_to_all(sent, 'dom', 0, 0, tiled=True)  15.1 us
    all_to_all x1, blocking collectives, body(): lax.all_to_all(coef.reshape(PARTS, ROWS, LANES), 'freq', 0, 0, tiled=True)  14.5 us
    all_to_all x1, blocking collectives, body(): incoming = lax.all_to_all(outgoing, 'dom', 0, 0, tiled=True)  12.6 us

profile of v1, /device:TPU:1, one launch (start us, length us, event | category | flops | bytes accessed | tf_op | source)
XLA Modules:
  0.0 109.7 jit_solution(11017879883783416926)
XLA Ops:
  0.6 0.0 slice-start
  0.6 0.7 slice-done
  1.4 0.0 copy-start.3
  1.4 0.0 copy-start.5
  1.4 0.0 copy-start.6
  1.4 0.0 copy-start.7
  1.4 15.1 %all_to_all.31.border_ref = f32[16,32,128]{2,1,0:T(8,128)S(1)} all-to-all(f32[16,32,128]{2,1,0:T(8,128)S(1)} %broadcast_in_dim.2), channel_id=1, replica_groups=mesh['dom'=16,'freq'=16] {'dom'}, dimensions={0} | all-to-all | bytes 524288 | tf_op jit(solution)/shard_map/all_to_all | solution.py:163
  16.5 0.0 copy-done.3
  16.5 0.0 copy-done.5
  16.5 0.0 copy-done.6
  16.5 0.0 copy-done.7
  16.5 16.8 %shard_map.103 = (f32[16,64,128]{2,1,0:T(8,128)S(1)}, f32[16,64,128]{2,1,0:T(8,128)S(1)}) custom-call(f32[32,2048]{1,0:T(8,128)S(1)} %copy-done.3, f32[16,32,128]{2,1,0:T(8,128)S(1)} %all_to_all.31.border_ref, s32[2,4096]{1,0:T(2,128)S(1)} %copy-done.5, f32[2,4096]{1,0:T(2,128)S(1)} %copy-done.6, f32[2,4096]{1,0:T(2,128)S(1)} %copy-done.7), custom_call_target="tpu_custom_call" | custom-call | tf_op jit(solution)/shard_map/pallas_call | solution.py:164
  33.3 0.0 copy-start.1
  33.4 12.6 %all_to_all.32 = f32[16,64,128]{2,1,0:T(8,128)S(1)} all-to-all(f32[16,64,128]{2,1,0:T(8,128)S(1)} %get-tuple-element.23), channel_id=1, replica_groups=mesh['dom'=16,'freq'=16] {'dom'}, dimensions={0} | all-to-all | bytes 1048576 | tf_op jit(solution)/shard_map/all_to_all | solution.py:170
  46.0 28.7 %all_to_all.33 = f32[16,64,128]{2,1,0:T(8,128)S(1)} all-to-all(f32[16,64,128]{2,1,0:T(8,128)S(1)} %fusion), channel_id=1, replica_groups=mesh['dom'=16,'freq'=16] {'freq'}, dimensions={0} | all-to-all | bytes 1048576 | tf_op jit(solution)/shard_map/all_to_all | solution.py:172
  74.7 0.0 copy-done.1
  74.7 0.0 copy-done
  74.7 1.0 shard_map.104
  75.7 0.0 copy-start.2
  75.7 14.5 %all_to_all.34.coef_ref = f32[16,32,128]{2,1,0:T(8,128)S(1)} all-to-all(f32[16,32,128]{2,1,0:T(8,128)S(1)} %bitcast.13), channel_id=1, replica_groups=mesh['dom'=16,'freq'=16] {'freq'}, dimensions={0} | all-to-all | bytes 524288 | tf_op jit(solution)/shard_map/all_to_all | solution.py:177
  90.3 0.0 copy-done.4
  90.3 1.2 %shard_map.105 = (f32[32,2048]{1,0:T(8,128)}, f32[32,2048]{1,0:T(8,128)S(1)}, f32[256,128]{1,0:T(8,128)S(1)}) custom-call(f32[16,32,128]{2,1,0:T(8,128)S(1)} %all_to_all.34.coef_ref, f32[32,2048]{1,0:T(8,128)S(1)} %copy-done.4, f32[32,2,2048]{2,1,0:T(2,128)S(1)} %bitcast.15), custom_call_target="tpu_custom_call" | custom-call | tf_op jit(solution)/shard_map/pallas_call | solution.py:178
  91.5 17.3 %all_to_all.35 = f32[256,1,128]{2,1,0:T(1,128)S(1)} all-to-all(f32[256,1,128]{2,1,0:T(1,128)S(1)} %bitcast.16), channel_id=1, replica_groups=mesh['dom'=16,'freq'=16] {'dom','freq'}, dimensions={0} | all-to-all | bytes 262144 | tf_op jit(solution)/shard_map/all_to_all | solution.py:181
  108.8 0.9 shard_map.106
  (6 shorter events, 0.1 us)
Async XLA Ops:
  0.6 0.7 slice-start
  1.4 15.1 %copy-start.3 = (f32[32,2048]{1,0:T(8,128)S(1)}, f32[32,2048]{1,0:T(8,128)}, u32[]{:S(2)}) copy-start(f32[32,2048]{1,0:T(8,128)} %volt_ref.1) | copy-start | bytes 786436
  1.4 15.1 %copy-start.5 = (s32[2,4096]{1,0:T(2,128)S(1)}, s32[2,4096]{1,0:T(2,128)}, u32[]{:S(2)}) copy-start(s32[2,4096]{1,0:T(2,128)} %term_ref.1) | copy-start | bytes 98308
  1.4 15.1 %copy-start.6 = (f32[2,4096]{1,0:T(2,128)S(1)}, f32[2,4096]{1,0:T(2,128)}, u32[]{:S(2)}) copy-start(f32[2,4096]{1,0:T(2,128)} %cur_ref.1) | copy-start | bytes 98308
  1.4 15.1 %copy-start.7 = (f32[2,4096]{1,0:T(2,128)S(1)}, f32[2,4096]{1,0:T(2,128)}, u32[]{:S(2)}) copy-start(f32[2,4096]{1,0:T(2,128)} %chg_ref.1) | copy-start | bytes 98308
  33.3 41.4 %copy-start.1 = (bf16[512,1024]{1,0:T(8,128)(2,1)S(1)}, bf16[512,1024]{1,0:T(8,128)(2,1)}, u32[]{:S(2)}) copy-start(bf16[512,1024]{1,0:T(8,128)(2,1)} %constant.33.clone.high_ref) | copy-start | bytes 3145732
  45.9 28.8 %copy-start = (bf16[512,1024]{1,0:T(8,128)(2,1)S(1)}, bf16[512,1024]{1,0:T(8,128)(2,1)}, u32[]{:S(2)}) copy-start(bf16[512,1024]{1,0:T(8,128)(2,1)} %constant.34.clone.low_ref) | copy-start | bytes 3145732
  74.7 15.5 %copy-start.4 = (f32[32,2048]{1,0:T(8,128)S(1)}, f32[32,2048]{1,0:T(8,128)}, u32[]{:S(2)}) copy-start(f32[32,2048]{1,0:T(8,128)} %src_ref.1) | copy-start | bytes 786436
  75.7 14.6 %copy-start.2 = (f32[16,2,2,2048]{3,2,1,0:T(2,128)S(1)}, f32[16,2,2,2048]{3,2,1,0:T(2,128)}, u32[]{:S(2)}) copy-start(f32[16,2,2,2048]{3,2,1,0:T(2,128)} %param.15) | copy-start | bytes 1572868

commit v2 on v1

v2 whole, which is shorter than its diff:
```python
import functools
import math

import jax
import jax.numpy as jnp
import ml_dtypes
import numpy as np
from jax import lax
from jax.experimental import pallas as pl
from jax.experimental.pallas import tpu as pltpu
from jax.sharding import PartitionSpec as P

S = 512
ROWS = 32
NPD = 2048
NE = 4096
NB = 128
PARTS = 16
LANES = 128
LOW = 512
SHIFT = 9
HIGHS = NPD // LOW
PER = LOW // LANES
TILE = 1024

trust_radius = 2.0
BF = jnp.bfloat16
F32 = jnp.float32


def transform_table():
    row = np.arange(S)
    harmonic = row // 2
    sine = (row % 2 == 1) & (harmonic > 0)
    order = np.where(harmonic == 0, np.where(row % 2 == 1, S // 2, 0), harmonic)
    phase = (order[:, None] * np.arange(S)[None, :] % S) * (2.0 * math.pi / S)
    values = np.where(sine[:, None], np.sin(phase), np.cos(phase))
    weight = np.where(harmonic == 0, math.sqrt(1.0 / S), math.sqrt(2.0 / S))
    forward = values * weight[:, None]
    pairs = forward.reshape(S // 2, 2, S)
    rate = 2.0 / S * np.arange(S // 2)
    derived = (np.stack([pairs[:, 1], -pairs[:, 0]], axis=1) * rate[:, None, None]).reshape(S, S)
    both = np.stack([forward.reshape(S, PARTS, ROWS), derived.reshape(S, PARTS, ROWS)], axis=2)
    return both.reshape(S, 2 * S)


def split(x):
    hi = x.astype(BF)
    return hi, (x - hi.astype(F32)).astype(BF)


def one_hot(low):
    rows = lax.broadcasted_iota(jnp.int32, (256, low.shape[1]), 0).astype(F32).astype(BF)
    parts = []
    for first in range(0, LOW, 256):
        offset = jnp.broadcast_to((low - first).astype(F32).astype(BF), rows.shape)
        parts.append(jnp.where(rows == offset, jnp.ones((), BF), jnp.zeros((), BF)))
    return jnp.concatenate(parts, axis=0)


def fill_table(blocks, table_ref):
    for a, block in enumerate(blocks):
        hi, lo = split(block)
        table_ref[a * ROWS : (a + 1) * ROWS, :] = hi
        table_ref[(HIGHS + a) * ROWS : (HIGHS + a + 1) * ROWS, :] = lo


def gather(table_ref, high, hot):
    found = jnp.dot(table_ref[...], hot, preferred_element_type=F32)
    value = jnp.zeros((ROWS, hot.shape[1]), F32)
    for a in range(HIGHS):
        part = found[a * ROWS : (a + 1) * ROWS] + found[(HIGHS + a) * ROWS : (HIGHS + a + 1) * ROWS]
        value = jnp.where(high == a, part, value)
    return value


def scatter(flows, highs, hots):
    sides = []
    for t in range(2):
        signed = flows if t == 0 else -flows
        sides += [
            jnp.concatenate(
                [signed * jnp.where(highs[t] == a, 1.0, 0.0).astype(BF) for a in range(HIGHS)], axis=0
            )
        ]
    return lax.dot_general(
        jnp.concatenate(sides, axis=1),
        jnp.concatenate(hots, axis=1),
        (((1,), (1,)), ((), ())),
        preferred_element_type=F32,
    )


def put_blocks(acc_ref, out_ref):
    for a in range(HIGHS):
        base = a * 4 * ROWS
        total = acc_ref[base : base + 2 * ROWS, :] + acc_ref[base + 2 * ROWS : base + 4 * ROWS, :]
        for k in range(PER):
            out_ref[a * PER + k] = total[:, k * LANES : (k + 1) * LANES]


def tiles():
    return [slice(first, first + TILE) for first in range(0, NE, TILE)]


def own_across_kernel(volt_ref, term_ref, across_ref, table_ref):
    fill_table([volt_ref[:, a * LOW : (a + 1) * LOW] for a in range(HIGHS)], table_ref)
    for cols in tiles():
        ends = []
        for t in range(2):
            node = term_ref[t : t + 1, cols]
            ends.append(gather(table_ref, node >> SHIFT, one_hot(node & (LOW - 1))))
        across_ref[:, cols] = ends[0] - ends[1]


def flow_kernel(border_ref, across_ref, term_ref, cur_ref, chg_ref, out_ref, flows_ref, table_ref, acc_ref):
    blocks = [
        jnp.concatenate([border_ref[a * PER + k] for k in range(PER)], axis=1) for a in range(HIGHS)
    ]
    fill_table(blocks, table_ref)
    for i, cols in enumerate(tiles()):
        highs, hots, ends = [], [], []
        for t in range(2):
            node = term_ref[t : t + 1, cols]
            highs.append((node >> SHIFT) - HIGHS)
            hots.append(one_hot(node & (LOW - 1)))
            ends.append(gather(table_ref, highs[t], hots[t]))
        across = across_ref[:, cols] + (ends[0] - ends[1])
        current = cur_ref[0:1, cols] * across + cur_ref[1:2, cols] * jnp.tanh(2.0 * across)
        charge = chg_ref[0:1, cols] * across + chg_ref[1:2, cols] * jnp.tanh(across)
        flows = jnp.concatenate(split(jnp.concatenate([current, charge], axis=0)), axis=0)
        flows_ref[:, cols] = flows
        part = scatter(flows, highs, hots)
        acc_ref[...] = part if i == 0 else acc_ref[...] + part
    put_blocks(acc_ref, out_ref)


def own_flow_kernel(flows_ref, term_ref, own_ref, acc_ref):
    for i, cols in enumerate(tiles()):
        highs, hots = [], []
        for t in range(2):
            node = term_ref[t : t + 1, cols]
            highs.append(node >> SHIFT)
            hots.append(one_hot(node & (LOW - 1)))
        part = scatter(flows_ref[:, cols], highs, hots)
        acc_ref[...] = part if i == 0 else acc_ref[...] + part
    put_blocks(acc_ref, own_ref)


def transform_kernel(flow_ref, high_ref, low_ref, out_ref):
    hi, lo = split(flow_ref[...])
    dot = functools.partial(jnp.dot, preferred_element_type=F32)
    out_ref[...] = dot(high_ref[...], hi) + (dot(high_ref[...], lo) + dot(low_ref[...], hi))


def step_kernel(coef_ref, src_ref, jac_ref, res_ref, raw_ref, sums_ref):
    even = lax.broadcasted_iota(jnp.int32, (ROWS, LANES), 0) % 2 == 0
    raw_sum = jnp.zeros((ROWS, LANES), F32)
    res_sum = jnp.zeros((ROWS, LANES), F32)
    for k in range(NPD // LANES):
        cols = slice(k * LANES, (k + 1) * LANES)
        res = coef_ref[k] - src_ref[:, cols]
        res_ref[:, cols] = res
        first = jnp.where(even, res, pltpu.roll(res, 1, 0))
        second = jnp.where(even, pltpu.roll(res, ROWS - 1, 0), res)
        raw = -(jac_ref[:, 0, cols] * first + jac_ref[:, 1, cols] * second)
        raw_ref[:, cols] = raw
        raw_sum += raw * raw
        res_sum += res * res
    raw_row = jnp.sum(raw_sum, axis=0, keepdims=True)
    res_row = jnp.sum(res_sum, axis=0, keepdims=True)
    half = lax.broadcasted_iota(jnp.int32, (1, LANES), 1) < LANES // 2
    row = jnp.where(half, raw_row + pltpu.roll(raw_row, LANES // 2, 1), res_row + pltpu.roll(res_row, LANES // 2, 1))
    sums_ref[...] = jnp.broadcast_to(row, sums_ref.shape)


def scale_kernel(raw_ref, sums_ref, out_ref, norm_ref):
    row = jnp.sum(sums_ref[...], axis=0, keepdims=True)
    half = lax.broadcasted_iota(jnp.int32, (1, LANES), 1) < LANES // 2
    raw_sum = jnp.sum(jnp.where(half, row, 0.0), axis=1, keepdims=True)
    res_sum = jnp.sum(jnp.where(half, 0.0, row), axis=1, keepdims=True)
    spread = jnp.sqrt(raw_sum / (S * NPD * PARTS) + 1e-06)
    out_ref[...] = raw_ref[...] * jnp.minimum(1.0, trust_radius / spread)
    norm_ref[...] = jnp.sqrt(res_sum)


def call(kernel, out_shapes, scratch=(), limit=24, flops=0, types=None):
    types = types or [F32] * len(out_shapes)
    return pl.pallas_call(
        kernel,
        out_shape=[jax.ShapeDtypeStruct(s, t) for s, t in zip(out_shapes, types, strict=True)],
        scratch_shapes=list(scratch),
        compiler_params=pltpu.CompilerParams(vmem_limit_bytes=limit * 2**20),
        cost_estimate=pl.CostEstimate(flops=flops, bytes_accessed=2**20, transcendentals=0) if flops else None,
    )


def body(voltages, sources, terminals, elem_current, elem_charge, jacobi):
    sent = jnp.broadcast_to(voltages[None, :, :NB], (PARTS, ROWS, NB))
    border = lax.all_to_all(sent, "dom", 0, 0, tiled=True)
    table_scratch = pltpu.VMEM((2 * HIGHS * ROWS, LOW), BF)
    acc_scratch = pltpu.VMEM((HIGHS * 4 * ROWS, LOW), F32)
    (across,) = call(own_across_kernel, [(ROWS, NE)], [table_scratch], 32, 4 * 10**9)(voltages, terminals)
    outgoing, flows = call(
        flow_kernel,
        [(PARTS, 2 * ROWS, LANES), (4 * ROWS, NE)],
        [table_scratch, acc_scratch],
        40,
        8 * 10**9,
        [F32, BF],
    )(border, across, terminals, elem_current, elem_charge)
    incoming = lax.all_to_all(outgoing, "dom", 0, 0, tiled=True)
    (own,) = call(own_flow_kernel, [(PARTS, 2 * ROWS, LANES)], [acc_scratch], 32, 6 * 10**9)(flows, terminals)
    own = own.at[0].add(jnp.sum(incoming, axis=0))
    flows = lax.all_to_all(own, "freq", 0, 0, tiled=True).reshape(2 * S, LANES)
    table = transform_table()
    high = table.astype(ml_dtypes.bfloat16)
    low = (table - high.astype(np.float64)).astype(ml_dtypes.bfloat16)
    (coef,) = call(transform_kernel, [(S, LANES)], )(flows, jnp.asarray(high), jnp.asarray(low))
    coef = lax.all_to_all(coef.reshape(PARTS, ROWS, LANES), "freq", 0, 0, tiled=True)
    residual, raw, sums = call(step_kernel, [(ROWS, NPD), (ROWS, NPD), (256, LANES)], )(
        coef, sources, jacobi.reshape(ROWS, 2, NPD)
    )
    sums = lax.all_to_all(sums, ("dom", "freq"), 0, 0, tiled=True)
    newton_step, norm = call(scale_kernel, [(ROWS, NPD), (1, 1)], )(raw, sums)
    return residual, newton_step, norm.reshape(())


def solution(mesh):
    placed = (
        P("freq", "dom"),
        P("freq", "dom"),
        P(None, "dom"),
        P(None, "dom"),
        P(None, "dom"),
        P("freq", None, None, "dom"),
    )
    return jax.shard_map(
        body,
        mesh=mesh,
        in_specs=placed,
        out_specs=(P("freq", "dom"), P("freq", "dom"), P()),
        check_vma=False,
    )
```

time: 110 us -> 103 us (0.936)
  blocking collectives: 88.2 us -> 60.5 us
  starting transfers between devices: 0 us -> 11.3 us
  waiting for transfers between devices: 0 us -> 8.84 us
  local copies, waits for them, and re-layouts: 0.78 us -> 3.68 us
  Pallas kernels: 19.9 us -> 17.5 us
    all_to_all x2 -> x0, blocking collectives: 27.6 us -> none  [the longest x1 15.1 us: body(): border = lax.all_to_all(sent, 'dom', 0, 0, tiled=True)]
    all_to_all x0 -> x2, starting transfers between devices: none -> 11.3 us  [the longest x1 7.72 us: body(): border = lax.all_to_all(sent, 'dom', 0, 0, tiled=True)]
    all_to_all x0 -> x2, waiting for transfers between devices: none -> 8.84 us  [the longest x1 5.14 us: body(): border = lax.all_to_all(sent, 'dom', 0, 0, tiled=True)]
    pallas_call x4 -> x6, Pallas kernels: 19.9 us -> 17.5 us  [the longest x1 7.52 us: body(): call(flow_kernel, [(PARTS, 2 * ROWS, LANES), (4 * ROWS, NE)], [table_scra...]
    unnamed x16 -> x20, local copies, waits for them, and re-layouts: 0.05 us -> 2.23 us
  transfers between devices with their start and end apart: 0 -> 2, of which waited for: 0 -> 2; matrix products, arithmetic and copies ran while one was open for 0% -> 0% of each run, Pallas kernels for 0% -> 7%
where the time goes in v2:
time: 103 us
  blocking collectives  60.5 us (59%)
  Pallas kernels  17.5 us (17%)
  starting transfers between devices  11.3 us (11%)
  waiting for transfers between devices  8.84 us (9%)
  local copies, waits for them, and re-layouts  3.68 us (4%)
    all_to_all x1, blocking collectives, body(): flows = lax.all_to_all(own, 'freq', 0, 0, tiled=True).reshape(2 * S, LANES)  28.6 us
    all_to_all x1, blocking collectives, body(): sums = lax.all_to_all(sums, ('dom', 'freq'), 0, 0, tiled=True)  17.3 us
    all_to_all x1, blocking collectives, body(): lax.all_to_all(coef.reshape(PARTS, ROWS, LANES), 'freq', 0, 0, tiled=True)  14.5 us
    all_to_all x1, starting transfers between devices, body(): border = lax.all_to_all(sent, 'dom', 0, 0, tiled=True)  7.72 us
    pallas_call x1, Pallas kernels, body(): call(flow_kernel, [(PARTS, 2 * ROWS, LANES), (4 * ROWS, NE)], [table_scra...  7.52 us
    all_to_all x1, waiting for transfers between devices, body(): border = lax.all_to_all(sent, 'dom', 0, 0, tiled=True)  5.14 us
    pallas_call x1, Pallas kernels, body(): call(own_flow_kernel, [(PARTS, 2 * ROWS, LANES)], [acc_scratch], 32, 6 *...  4.52 us
    all_to_all x1, waiting for transfers between devices, body(): incoming = lax.all_to_all(outgoing, 'dom', 0, 0, tiled=True)  3.7 us
  transfers between devices with their start and end apart: 2, of which 2 were waited for; matrix products, arithmetic and copies ran while one was open for 0% of the time, Pallas kernels for 7%

profile of v2, /device:TPU:1, one launch (start us, length us, event | category | flops | bytes accessed | tf_op | source)
XLA Modules:
  0.0 102.5 jit_solution(7150050669192545242)
XLA Ops:
  0.6 0.0 slice-start
  0.6 0.7 slice-done
  1.4 0.7 broadcast_in_dim.2
  2.1 7.7 %all-to-all-start = ((f32[16,32,128]{2,1,0:T(8,128)}), f32[16,32,128]{2,1,0:T(8,128)S(1)}, u32[]{:S(2)}, u32[]{:S(2)}) async-start(f32[16,32,128]{2,1,0:T(8,128)} %broadcast_in_dim.2), calls=%async_computation | async-start | bytes 524288 | tf_op jit(solution)/shard_map/all_to_all | solution.py:200
  9.8 0.0 copy-start.5
  9.8 0.0 copy-start.6
  9.9 2.4 %shard_map.103.across_ref = f32[32,4096]{1,0:T(8,128)S(1)} custom-call(f32[32,2048]{1,0:T(8,128)S(1)} %copy-done.4, s32[2,4096]{1,0:T(2,128)S(1)} %copy-done.7), custom_call_target="tpu_custom_call" | custom-call | flops 4000000000 | bytes 1048576 | tf_op jit(solution)/shard_map/pallas_call | solution.py:203
  12.2 5.1 %all-to-all-done.border_ref = f32[16,32,128]{2,1,0:T(8,128)S(1)} async-done(((f32[16,32,128]{2,1,0:T(8,128)}), f32[16,32,128]{2,1,0:T(8,128)S(1)}, u32[]{:S(2)}, u32[]{:S(2)}) %all-to-all-start) | async-done | bytes 262176 | tf_op jit(solution)/shard_map/all_to_all | solution.py:200
  17.4 0.0 copy-done.6
  17.4 7.5 %shard_map.104 = (f32[16,64,128]{2,1,0:T(8,128)}, bf16[128,4096]{1,0:T(8,128)(2,1)S(1)}) custom-call(f32[16,32,128]{2,1,0:T(8,128)S(1)} %all-to-all-done.border_ref, f32[32,4096]{1,0:T(8,128)S(1)} %shard_map.103.across_ref, s32[2,4096]{1,0:T(2,128)S(1)} %copy-done.7, f32[2,4096]{1,0:T(2,128)S(1)} %copy-done.5, f32[2,4096]{1,0:T(2,128)S(1)} %copy-done.6), custom_call_target="tpu_custom_call" | custom-call | flops 8000000000 | bytes 1048576 | tf_op jit(solution)/shard_map/pallas_call | solution.py:204
  24.9 1.0 copy-done.8
  25.9 3.6 %all-to-all-start.1 = ((f32[16,64,128]{2,1,0:T(8,128)}), f32[16,64,128]{2,1,0:T(8,128)S(1)}, u32[]{:S(2)}, u32[]{:S(2)}) async-start(f32[16,64,128]{2,1,0:T(8,128)} %get-tuple-element.23), calls=%async_computation.1 | async-start | bytes 1048576 | tf_op jit(solution)/shard_map/all_to_all | solution.py:212
  29.4 0.0 copy-start.9
  29.4 1.2 %copy-done.9 = bf16[128,4096]{1,0:T(8,128)(2,1)S(1)} copy-done((bf16[128,4096]{1,0:T(8,128)(2,1)S(1)}, bf16[128,4096]{1,0:T(8,128)(2,1)}, u32[]{:S(2)}) %copy-start.9) | copy-done | bytes 1048600
  30.7 4.5 %shard_map.105 = f32[16,64,128]{2,1,0:T(8,128)S(1)} custom-call(bf16[128,4096]{1,0:T(8,128)(2,1)S(1)} %copy-done.9, s32[2,4096]{1,0:T(2,128)S(1)} %copy-done.7), custom_call_target="tpu_custom_call" | custom-call | flops 6000000000 | bytes 1048576 | tf_op jit(solution)/shard_map/pallas_call | solution.py:213
  35.2 0.0 copy-start
  35.2 3.7 %all-to-all-done.1 = f32[16,64,128]{2,1,0:T(8,128)S(1)} async-done(((f32[16,64,128]{2,1,0:T(8,128)}), f32[16,64,128]{2,1,0:T(8,128)S(1)}, u32[]{:S(2)}, u32[]{:S(2)}) %all-to-all-start.1) | async-done | bytes 524320 | tf_op jit(solution)/shard_map/all_to_all | solution.py:212
  38.9 28.6 %all_to_all.31 = f32[16,64,128]{2,1,0:T(8,128)S(1)} all-to-all(f32[16,64,128]{2,1,0:T(8,128)S(1)} %fusion), channel_id=1, replica_groups=mesh['dom'=16,'freq'=16] {'freq'}, dimensions={0} | all-to-all | bytes 1048576 | tf_op jit(solution)/shard_map/all_to_all | solution.py:215
  67.6 1.0 shard_map.106
  68.6 0.0 copy-start.2
  68.6 14.5 %all_to_all.32.coef_ref = f32[16,32,128]{2,1,0:T(8,128)S(1)} all-to-all(f32[16,32,128]{2,1,0:T(8,128)S(1)} %bitcast.11), channel_id=1, replica_groups=mesh['dom'=16,'freq'=16] {'freq'}, dimensions={0} | all-to-all | bytes 524288 | tf_op jit(solution)/shard_map/all_to_all | solution.py:220
  83.1 1.2 %shard_map.107 = (f32[32,2048]{1,0:T(8,128)}, f32[32,2048]{1,0:T(8,128)S(1)}, f32[256,128]{1,0:T(8,128)S(1)}) custom-call(f32[16,32,128]{2,1,0:T(8,128)S(1)} %all_to_all.32.coef_ref, f32[32,2048]{1,0:T(8,128)S(1)} %copy-done.3, f32[32,2,2048]{2,1,0:T(2,128)S(1)} %bitcast.13), custom_call_target="tpu_custom_call" | custom-call | tf_op jit(solution)/shard_map/pallas_call | solution.py:221
  84.4 17.3 %all_to_all.33 = f32[256,1,128]{2,1,0:T(1,128)S(1)} all-to-all(f32[256,1,128]{2,1,0:T(1,128)S(1)} %bitcast.14), channel_id=1, replica_groups=mesh['dom'=16,'freq'=16] {'dom','freq'}, dimensions={0} | all-to-all | bytes 262144 | tf_op jit(solution)/shard_map/all_to_all | solution.py:224
  101.7 0.9 shard_map.108
  (14 shorter events, 0.1 us)
Async XLA Ops:
  0.6 0.7 slice-start
  2.1 7.7 %copy-start.4 = (f32[32,2048]{1,0:T(8,128)S(1)}, f32[32,2048]{1,0:T(8,128)}, u32[]{:S(2)}) copy-start(f32[32,2048]{1,0:T(8,128)} %volt_ref.1) | copy-start | bytes 786436
  2.1 7.7 %copy-start.7 = (s32[2,4096]{1,0:T(2,128)S(1)}, s32[2,4096]{1,0:T(2,128)}, u32[]{:S(2)}) copy-start(s32[2,4096]{1,0:T(2,128)} %term_ref.5) | copy-start | bytes 98308
  2.1 15.3 %all-to-all-start = ((f32[16,32,128]{2,1,0:T(8,128)}), f32[16,32,128]{2,1,0:T(8,128)S(1)}, u32[]{:S(2)}, u32[]{:S(2)}) async-start(f32[16,32,128]{2,1,0:T(8,128)} %broadcast_in_dim.2), calls=%async_computation | async-start | bytes 524288 | tf_op jit(solution)/shard_map/all_to_all | solution.py:200
  9.8 7.5 %copy-start.5 = (f32[2,4096]{1,0:T(2,128)S(1)}, f32[2,4096]{1,0:T(2,128)}, u32[]{:S(2)}) copy-start(f32[2,4096]{1,0:T(2,128)} %cur_ref.1) | copy-start | bytes 98308
  9.8 7.5 %copy-start.6 = (f32[2,4096]{1,0:T(2,128)S(1)}, f32[2,4096]{1,0:T(2,128)}, u32[]{:S(2)}) copy-start(f32[2,4096]{1,0:T(2,128)} %chg_ref.1) | copy-start | bytes 98308
  24.9 1.0 copy-start.8
  25.9 13.0 %all-to-all-start.1 = ((f32[16,64,128]{2,1,0:T(8,128)}), f32[16,64,128]{2,1,0:T(8,128)S(1)}, u32[]{:S(2)}, u32[]{:S(2)}) async-start(f32[16,64,128]{2,1,0:T(8,128)} %get-tuple-element.23), calls=%async_computation.1 | async-start | bytes 1048576 | tf_op jit(solution)/shard_map/all_to_all | solution.py:212
  29.4 1.2 %copy-start.9 = (bf16[128,4096]{1,0:T(8,128)(2,1)S(1)}, bf16[128,4096]{1,0:T(8,128)(2,1)}, u32[]{:S(2)}) copy-start(bf16[128,4096]{1,0:T(8,128)(2,1)} %copy-done.8) | copy-start | bytes 3145732
  30.7 36.9 %copy-start.1 = (bf16[512,1024]{1,0:T(8,128)(2,1)S(1)}, bf16[512,1024]{1,0:T(8,128)(2,1)}, u32[]{:S(2)}) copy-start(bf16[512,1024]{1,0:T(8,128)(2,1)} %constant.33.clone.high_ref) | copy-start | bytes 3145732
  35.2 32.4 %copy-start = (bf16[512,1024]{1,0:T(8,128)(2,1)S(1)}, bf16[512,1024]{1,0:T(8,128)(2,1)}, u32[]{:S(2)}) copy-start(bf16[512,1024]{1,0:T(8,128)(2,1)} %constant.34.clone.low_ref) | copy-start | bytes 3145732
  67.6 15.5 %copy-start.3 = (f32[32,2048]{1,0:T(8,128)S(1)}, f32[32,2048]{1,0:T(8,128)}, u32[]{:S(2)}) copy-start(f32[32,2048]{1,0:T(8,128)} %src_ref.1) | copy-start | bytes 786436
  68.6 14.6 %copy-start.2 = (f32[16,2,2,2048]{3,2,1,0:T(2,128)S(1)}, f32[16,2,2,2048]{3,2,1,0:T(2,128)}, u32[]{:S(2)}) copy-start(f32[16,2,2,2048]{3,2,1,0:T(2,128)} %param.15) | copy-start | bytes 1572868

commit v3 on v2

--- a/solution.py
+++ b/solution.py
@@ -74,6 +74,22 @@
     return value
 
 
+def lane_gather(border_ref, node):
+    groups = range(0, ROWS, 8)
+    columns = []
+    for first in range(0, node.shape[1], LANES):
+        here = jnp.broadcast_to(node[:, first : first + LANES], (8, LANES))
+        block, lane = (here >> 7) - PARTS, here & (LANES - 1)
+        values = [jnp.zeros((8, LANES), F32) for _ in groups]
+        for p in range(PARTS):
+            match = block == p
+            for i, r in enumerate(groups):
+                found = jnp.take_along_axis(border_ref[p, r : r + 8, :], lane, axis=1)
+                values[i] = jnp.where(match, found, values[i])
+        columns.append(jnp.concatenate(values, axis=0))
+    return jnp.concatenate(columns, axis=1)
+
+
 def scatter(flows, highs, hots):
     sides = []
     for t in range(2):
@@ -113,36 +129,57 @@
         across_ref[:, cols] = ends[0] - ends[1]
 
 
-def flow_kernel(border_ref, across_ref, term_ref, cur_ref, chg_ref, out_ref, flows_ref, table_ref, acc_ref):
+def flow_kernel(border_ref, across_ref, term_ref, cur_ref, chg_ref, out_ref, flows_ref, table_ref, acc_ref, keep_ref, sems):
     blocks = [
         jnp.concatenate([border_ref[a * PER + k] for k in range(PER)], axis=1) for a in range(HIGHS)
     ]
     fill_table(blocks, table_ref)
-    for i, cols in enumerate(tiles()):
+    copies = []
+
+    def front(i):
+        cols = tiles()[i]
         highs, hots, ends = [], [], []
         for t in range(2):
             node = term_ref[t : t + 1, cols]
             highs.append((node >> SHIFT) - HIGHS)
             hots.append(one_hot(node & (LOW - 1)))
-            ends.append(gather(table_ref, highs[t], hots[t]))
+            ends.append(lane_gather(border_ref, node) if i else gather(table_ref, highs[t], hots[t]))
         across = across_ref[:, cols] + (ends[0] - ends[1])
         current = cur_ref[0:1, cols] * across + cur_ref[1:2, cols] * jnp.tanh(2.0 * across)
         charge = chg_ref[0:1, cols] * across + chg_ref[1:2, cols] * jnp.tanh(across)
         flows = jnp.concatenate(split(jnp.concatenate([current, charge], axis=0)), axis=0)
-        flows_ref[:, cols] = flows
-        part = scatter(flows, highs, hots)
+        keep_ref[:, cols] = flows
+        copies.append(pltpu.make_async_copy(keep_ref.at[:, cols], flows_ref.at[:, cols], sems.at[i]))
+        copies[i].start()
+        return flows, highs, hots
+
+    count = NE // TILE
+    now = front(0)
+    for i in range(count):
+        later = front(i + 1) if i + 1 < count else None
+        part = scatter(*now)
         acc_ref[...] = part if i == 0 else acc_ref[...] + part
+        now = later
     put_blocks(acc_ref, out_ref)
-
-
-def own_flow_kernel(flows_ref, term_ref, own_ref, acc_ref):
+    for copy in copies:
+        copy.wait()
+
+
+def own_flow_kernel(flows_ref, term_ref, own_ref, acc_ref, keep_ref, sems):
+    copies = [
+        pltpu.make_async_copy(flows_ref.at[:, cols], keep_ref.at[:, cols], sems.at[i])
+        for i, cols in enumerate(tiles())
+    ]
+    for copy in copies:
+        copy.start()
     for i, cols in enumerate(tiles()):
         highs, hots = [], []
         for t in range(2):
             node = term_ref[t : t + 1, cols]
             highs.append(node >> SHIFT)
             hots.append(one_hot(node & (LOW - 1)))
-        part = scatter(flows_ref[:, cols], highs, hots)
+        copies[i].wait()
+        part = scatter(keep_ref[:, cols], highs, hots)
         acc_ref[...] = part if i == 0 else acc_ref[...] + part
     put_blocks(acc_ref, own_ref)
 
@@ -184,33 +221,63 @@
     norm_ref[...] = jnp.sqrt(res_sum)
 
 
-def call(kernel, out_shapes, scratch=(), limit=24, flops=0, types=None):
+def call(kernel, out_shapes, scratch=(), limit=24, flops=0, types=None, inside=None, outside=None):
     types = types or [F32] * len(out_shapes)
+    spaces = {}
+    if inside:
+        spaces["in_specs"] = [pl.BlockSpec(memory_space=m) for m in inside]
+    if outside:
+        spaces["out_specs"] = [pl.BlockSpec(memory_space=m) for m in outside]
     return pl.pallas_call(
         kernel,
         out_shape=[jax.ShapeDtypeStruct(s, t) for s, t in zip(out_shapes, types, strict=True)],
         scratch_shapes=list(scratch),
         compiler_params=pltpu.CompilerParams(vmem_limit_bytes=limit * 2**20),
         cost_estimate=pl.CostEstimate(flops=flops, bytes_accessed=2**20, transcendentals=0) if flops else None,
-    )
+        **spaces,
+    )
+
+
+def repeat_kernel(block_ref, out_ref):
+    block = block_ref[...]
+    for p in range(PARTS):
+        out_ref[p] = block
 
 
 def body(voltages, sources, terminals, elem_current, elem_charge, jacobi):
-    sent = jnp.broadcast_to(voltages[None, :, :NB], (PARTS, ROWS, NB))
+    sent = pl.pallas_call(
+        repeat_kernel,
+        out_shape=jax.ShapeDtypeStruct((PARTS, ROWS, NB), F32),
+        grid=(1,),
+        in_specs=[pl.BlockSpec((ROWS, NB), lambda i: (0, 0))],
+        out_specs=pl.BlockSpec((PARTS, ROWS, NB), lambda i: (0, 0, 0)),
+    )(voltages)
     border = lax.all_to_all(sent, "dom", 0, 0, tiled=True)
     table_scratch = pltpu.VMEM((2 * HIGHS * ROWS, LOW), BF)
     acc_scratch = pltpu.VMEM((HIGHS * 4 * ROWS, LOW), F32)
+    keep = [pltpu.VMEM((4 * ROWS, NE), BF), pltpu.SemaphoreType.DMA((NE // TILE,))]
     (across,) = call(own_across_kernel, [(ROWS, NE)], [table_scratch], 32, 4 * 10**9)(voltages, terminals)
     outgoing, flows = call(
         flow_kernel,
         [(PARTS, 2 * ROWS, LANES), (4 * ROWS, NE)],
-        [table_scratch, acc_scratch],
+        [table_scratch, acc_scratch, *keep],
         40,
         8 * 10**9,
         [F32, BF],
+        None,
+        [pltpu.VMEM, pltpu.HBM],
     )(border, across, terminals, elem_current, elem_charge)
+    own_call = call(
+        own_flow_kernel,
+        [(PARTS, 2 * ROWS, LANES)],
+        [acc_scratch, *keep],
+        32,
+        6 * 10**9,
+        None,
+        [pltpu.HBM, pltpu.VMEM],
+    )
+    (own,) = own_call(flows, terminals)
     incoming = lax.all_to_all(outgoing, "dom", 0, 0, tiled=True)
-    (own,) = call(own_flow_kernel, [(PARTS, 2 * ROWS, LANES)], [acc_scratch], 32, 6 * 10**9)(flows, terminals)
     own = own.at[0].add(jnp.sum(incoming, axis=0))
     flows = lax.all_to_all(own, "freq", 0, 0, tiled=True).reshape(2 * S, LANES)
     table = transform_table()

time: 103 us -> 104 us (level)
  Pallas kernels: 17.5 us -> 20.4 us
  local copies, waits for them, and re-layouts: 3.68 us -> 2.23 us
    pallas_call x1 -> x2, Pallas kernels: 4.52 us -> 6.88 us  [the longest x1 5.43 us: body(): own, = own_call(flows, terminals)]
  transfers between devices with their start and end apart: 2 -> 2, of which waited for: 2 -> 2; matrix products, arithmetic and copies ran while one was open for 0% -> 0% of each run, Pallas kernels for 7% -> 8%
where the time goes in v3:
time: 104 us
  blocking collectives  61 us (59%)
  Pallas kernels  20.4 us (20%)
  starting transfers between devices  11.3 us (11%)
  waiting for transfers between devices  7.92 us (8%)
  local copies, waits for them, and re-layouts  2.23 us (2%)
    all_to_all x1, blocking collectives, body(): flows = lax.all_to_all(own, 'freq', 0, 0, tiled=True).reshape(2 * S, LANES)  28.6 us
    all_to_all x1, blocking collectives, body(): sums = lax.all_to_all(sums, ('dom', 'freq'), 0, 0, tiled=True)  17.8 us
    all_to_all x1, blocking collectives, body(): lax.all_to_all(coef.reshape(PARTS, ROWS, LANES), 'freq', 0, 0, tiled=True)  14.5 us
    pallas_call x1, Pallas kernels, body(): call(flow_kernel, [(PARTS, 2 * ROWS, LANES), (4 * ROWS, NE)], [table_scra...  8.06 us
    all_to_all x1, starting transfers between devices, body(): border = lax.all_to_all(sent, 'dom', 0, 0, tiled=True)  7.72 us
    pallas_call x1, Pallas kernels, body(): own, = own_call(flows, terminals)  5.43 us
    all_to_all x1, waiting for transfers between devices, body(): border = lax.all_to_all(sent, 'dom', 0, 0, tiled=True)  5.14 us
    all_to_all x1, starting transfers between devices, body(): incoming = lax.all_to_all(outgoing, 'dom', 0, 0, tiled=True)  3.57 us
  transfers between devices with their start and end apart: 2, of which 2 were waited for; matrix products, arithmetic and copies ran while one was open for 0% of the time, Pallas kernels for 8%

profile of v3, /device:TPU:1, one launch (start us, length us, event | category | flops | bytes accessed | tf_op | source)
XLA Modules:
  0.0 103.6 jit_solution(3207705145922281364)
XLA Ops:
  0.6 1.4 %shard_map.103 = f32[16,32,128]{2,1,0:T(8,128)} custom-call(f32[32,2048]{1,0:T(8,128)} %volt_ref.1), custom_call_target="tpu_custom_call" | custom-call | tf_op jit(solution)/shard_map/pallas_call | solution.py:248
  2.1 7.7 %all-to-all-start = ((f32[16,32,128]{2,1,0:T(8,128)}), f32[16,32,128]{2,1,0:T(8,128)S(1)}, u32[]{:S(2)}, u32[]{:S(2)}) async-start(f32[16,32,128]{2,1,0:T(8,128)} %shard_map.103), calls=%async_computation | async-start | bytes 524288 | tf_op jit(solution)/shard_map/all_to_all | solution.py:255
  9.8 0.0 copy-done.3
  9.8 0.0 copy-done.7
  9.8 0.0 copy-start.5
  9.8 0.0 copy-start.6
  9.8 2.4 %shard_map.104.across_ref = f32[32,4096]{1,0:T(8,128)S(1)} custom-call(f32[32,2048]{1,0:T(8,128)S(1)} %copy-done.3, s32[2,4096]{1,0:T(2,128)S(1)} %copy-done.7), custom_call_target="tpu_custom_call" | custom-call | flops 4000000000 | bytes 1048576 | tf_op jit(solution)/shard_map/pallas_call | solution.py:259
  12.2 5.1 %all-to-all-done.border_ref = f32[16,32,128]{2,1,0:T(8,128)S(1)} async-done(((f32[16,32,128]{2,1,0:T(8,128)}), f32[16,32,128]{2,1,0:T(8,128)S(1)}, u32[]{:S(2)}, u32[]{:S(2)}) %all-to-all-start) | async-done | bytes 262176 | tf_op jit(solution)/shard_map/all_to_all | solution.py:255
  17.3 0.0 copy-done.5
  17.4 0.0 copy-done.6
  17.4 8.1 %shard_map.105 = (f32[16,64,128]{2,1,0:T(8,128)}, bf16[128,4096]{1,0:T(8,128)(2,1)S(1)}) custom-call(f32[16,32,128]{2,1,0:T(8,128)S(1)} %all-to-all-done.border_ref, f32[32,4096]{1,0:T(8,128)S(1)} %shard_map.104.across_ref, s32[2,4096]{1,0:T(2,128)S(1)} %copy-done.7, f32[2,4096]{1,0:T(2,128)S(1)} %copy-done.5, f32[2,4096]{1,0:T(2,128)S(1)} %copy-done.6), custom_call_target="tpu_custom_call" | custom-call | flops 8000000000 | bytes 1048576 | tf_op jit(solution)/shard_map/pallas_call | solution.py:260
  25.4 1.0 copy-done.8
  26.4 3.6 %all-to-all-start.1 = ((f32[16,64,128]{2,1,0:T(8,128)}), f32[16,64,128]{2,1,0:T(8,128)S(1)}, u32[]{:S(2)}, u32[]{:S(2)}) async-start(f32[16,64,128]{2,1,0:T(8,128)} %get-tuple-element.23), calls=%async_computation.1 | async-start | bytes 1048576 | tf_op jit(solution)/shard_map/all_to_all | solution.py:280
  30.0 1.2 %copy-done.9 = bf16[128,4096]{1,0:T(8,128)(2,1)S(1)} copy-done((bf16[128,4096]{1,0:T(8,128)(2,1)S(1)}, bf16[128,4096]{1,0:T(8,128)(2,1)}, u32[]{:S(2)}) %copy-start.9) | copy-done | bytes 1048600
  31.2 5.4 %shard_map.106 = f32[16,64,128]{2,1,0:T(8,128)S(1)} custom-call(bf16[128,4096]{1,0:T(8,128)(2,1)S(1)} %copy-done.9, s32[2,4096]{1,0:T(2,128)S(1)} %copy-done.7), custom_call_target="tpu_custom_call" | custom-call | flops 6000000000 | bytes 1048576 | tf_op jit(solution)/shard_map/pallas_call | solution.py:279
  36.7 0.0 copy-start
  36.7 2.8 %all-to-all-done.1 = f32[16,64,128]{2,1,0:T(8,128)S(1)} async-done(((f32[16,64,128]{2,1,0:T(8,128)}), f32[16,64,128]{2,1,0:T(8,128)S(1)}, u32[]{:S(2)}, u32[]{:S(2)}) %all-to-all-start.1) | async-done | bytes 524320 | tf_op jit(solution)/shard_map/all_to_all | solution.py:280
  39.5 28.6 %all_to_all.31 = f32[16,64,128]{2,1,0:T(8,128)S(1)} all-to-all(f32[16,64,128]{2,1,0:T(8,128)S(1)} %fusion), channel_id=1, replica_groups=mesh['dom'=16,'freq'=16] {'freq'}, dimensions={0} | all-to-all | bytes 1048576 | tf_op jit(solution)/shard_map/all_to_all | solution.py:282
  68.1 1.0 shard_map.107
  69.1 0.0 copy-start.2
  69.1 14.5 %all_to_all.32.coef_ref = f32[16,32,128]{2,1,0:T(8,128)S(1)} all-to-all(f32[16,32,128]{2,1,0:T(8,128)S(1)} %bitcast.11), channel_id=1, replica_groups=mesh['dom'=16,'freq'=16] {'freq'}, dimensions={0} | all-to-all | bytes 524288 | tf_op jit(solution)/shard_map/all_to_all | solution.py:287
  83.7 1.2 %shard_map.108 = (f32[32,2048]{1,0:T(8,128)}, f32[32,2048]{1,0:T(8,128)S(1)}, f32[256,128]{1,0:T(8,128)S(1)}) custom-call(f32[16,32,128]{2,1,0:T(8,128)S(1)} %all_to_all.32.coef_ref, f32[32,2048]{1,0:T(8,128)S(1)} %copy-done.4, f32[32,2,2048]{2,1,0:T(2,128)S(1)} %bitcast.13), custom_call_target="tpu_custom_call" | custom-call | tf_op jit(solution)/shard_map/pallas_call | solution.py:288
  84.9 17.8 %all_to_all.33 = f32[256,1,128]{2,1,0:T(1,128)S(1)} all-to-all(f32[256,1,128]{2,1,0:T(1,128)S(1)} %bitcast.14), channel_id=1, replica_groups=mesh['dom'=16,'freq'=16] {'dom','freq'}, dimensions={0} | all-to-all | bytes 262144 | tf_op jit(solution)/shard_map/all_to_all | solution.py:291
  102.7 0.9 shard_map.109
  (12 shorter events, 0.1 us)
Async XLA Ops:
  2.1 7.7 %copy-start.3 = (f32[32,2048]{1,0:T(8,128)S(1)}, f32[32,2048]{1,0:T(8,128)}, u32[]{:S(2)}) copy-start(f32[32,2048]{1,0:T(8,128)} %volt_ref.1) | copy-start | bytes 786436
  2.1 7.7 %copy-start.7 = (s32[2,4096]{1,0:T(2,128)S(1)}, s32[2,4096]{1,0:T(2,128)}, u32[]{:S(2)}) copy-start(s32[2,4096]{1,0:T(2,128)} %term_ref.5) | copy-start | bytes 98308
  2.1 15.3 %all-to-all-start = ((f32[16,32,128]{2,1,0:T(8,128)}), f32[16,32,128]{2,1,0:T(8,128)S(1)}, u32[]{:S(2)}, u32[]{:S(2)}) async-start(f32[16,32,128]{2,1,0:T(8,128)} %shard_map.103), calls=%async_computation | async-start | bytes 524288 | tf_op jit(solution)/shard_map/all_to_all | solution.py:255
  9.8 7.5 %copy-start.5 = (f32[2,4096]{1,0:T(2,128)S(1)}, f32[2,4096]{1,0:T(2,128)}, u32[]{:S(2)}) copy-start(f32[2,4096]{1,0:T(2,128)} %cur_ref.1) | copy-start | bytes 98308
  9.8 7.5 %copy-start.6 = (f32[2,4096]{1,0:T(2,128)S(1)}, f32[2,4096]{1,0:T(2,128)}, u32[]{:S(2)}) copy-start(f32[2,4096]{1,0:T(2,128)} %chg_ref.1) | copy-start | bytes 98308
  25.4 1.0 copy-start.8
  26.4 13.0 %all-to-all-start.1 = ((f32[16,64,128]{2,1,0:T(8,128)}), f32[16,64,128]{2,1,0:T(8,128)S(1)}, u32[]{:S(2)}, u32[]{:S(2)}) async-start(f32[16,64,128]{2,1,0:T(8,128)} %get-tuple-element.23), calls=%async_computation.1 | async-start | bytes 1048576 | tf_op jit(solution)/shard_map/all_to_all | solution.py:280
  30.0 1.2 %copy-start.9 = (bf16[128,4096]{1,0:T(8,128)(2,1)S(1)}, bf16[128,4096]{1,0:T(8,128)(2,1)}, u32[]{:S(2)}) copy-start(bf16[128,4096]{1,0:T(8,128)(2,1)} %copy-done.8) | copy-start | bytes 3145732
  31.2 36.9 %copy-start.1 = (bf16[512,1024]{1,0:T(8,128)(2,1)S(1)}, bf16[512,1024]{1,0:T(8,128)(2,1)}, u32[]{:S(2)}) copy-start(bf16[512,1024]{1,0:T(8,128)(2,1)} %constant.33.clone.high_ref) | copy-start | bytes 3145732
  36.7 31.5 %copy-start = (bf16[512,1024]{1,0:T(8,128)(2,1)S(1)}, bf16[512,1024]{1,0:T(8,128)(2,1)}, u32[]{:S(2)}) copy-start(bf16[512,1024]{1,0:T(8,128)(2,1)} %constant.34.clone.low_ref) | copy-start | bytes 3145732
  68.1 15.5 %copy-start.4 = (f32[32,2048]{1,0:T(8,128)S(1)}, f32[32,2048]{1,0:T(8,128)}, u32[]{:S(2)}) copy-start(f32[32,2048]{1,0:T(8,128)} %src_ref.1) | copy-start | bytes 786436
  69.1 14.6 %copy-start.2 = (f32[16,2,2,2048]{3,2,1,0:T(2,128)S(1)}, f32[16,2,2,2048]{3,2,1,0:T(2,128)}, u32[]{:S(2)}) copy-start(f32[16,2,2,2048]{3,2,1,0:T(2,128)} %param.15) | copy-start | bytes 1572868

commit v4 on v2

--- a/solution.py
+++ b/solution.py
@@ -74,6 +74,22 @@
     return value
 
 
+def lane_gather(border_ref, node):
+    groups = range(0, ROWS, 8)
+    columns = []
+    for first in range(0, node.shape[1], LANES):
+        here = jnp.broadcast_to(node[:, first : first + LANES], (8, LANES))
+        block, lane = (here >> 7) - PARTS, here & (LANES - 1)
+        values = [jnp.zeros((8, LANES), F32) for _ in groups]
+        for p in range(PARTS):
+            match = block == p
+            for i, r in enumerate(groups):
+                found = jnp.take_along_axis(border_ref[p, r : r + 8, :], lane, axis=1)
+                values[i] = jnp.where(match, found, values[i])
+        columns.append(jnp.concatenate(values, axis=0))
+    return jnp.concatenate(columns, axis=1)
+
+
 def scatter(flows, highs, hots):
     sides = []
     for t in range(2):
@@ -113,37 +129,55 @@
         across_ref[:, cols] = ends[0] - ends[1]
 
 
-def flow_kernel(border_ref, across_ref, term_ref, cur_ref, chg_ref, out_ref, flows_ref, table_ref, acc_ref):
+def flows_of(across, cur_ref, chg_ref, cols):
+    current = cur_ref[0:1, cols] * across + cur_ref[1:2, cols] * jnp.tanh(2.0 * across)
+    charge = chg_ref[0:1, cols] * across + chg_ref[1:2, cols] * jnp.tanh(across)
+    return jnp.concatenate(split(jnp.concatenate([current, charge], axis=0)), axis=0)
+
+
+def add_up(front, acc_ref):
+    count = NE // TILE
+    now = front(0)
+    for i in range(count):
+        later = front(i + 1) if i + 1 < count else None
+        part = scatter(*now)
+        acc_ref[...] = part if i == 0 else acc_ref[...] + part
+        now = later
+
+
+def flow_kernel(border_ref, own_ref, term_ref, cur_ref, chg_ref, out_ref, across_ref, table_ref, acc_ref):
     blocks = [
         jnp.concatenate([border_ref[a * PER + k] for k in range(PER)], axis=1) for a in range(HIGHS)
     ]
     fill_table(blocks, table_ref)
-    for i, cols in enumerate(tiles()):
+
+    def front(i):
+        cols = tiles()[i]
         highs, hots, ends = [], [], []
         for t in range(2):
             node = term_ref[t : t + 1, cols]
             highs.append((node >> SHIFT) - HIGHS)
             hots.append(one_hot(node & (LOW - 1)))
-            ends.append(gather(table_ref, highs[t], hots[t]))
-        across = across_ref[:, cols] + (ends[0] - ends[1])
-        current = cur_ref[0:1, cols] * across + cur_ref[1:2, cols] * jnp.tanh(2.0 * across)
-        charge = chg_ref[0:1, cols] * across + chg_ref[1:2, cols] * jnp.tanh(across)
-        flows = jnp.concatenate(split(jnp.concatenate([current, charge], axis=0)), axis=0)
-        flows_ref[:, cols] = flows
-        part = scatter(flows, highs, hots)
-        acc_ref[...] = part if i == 0 else acc_ref[...] + part
+            ends.append(lane_gather(border_ref, node) if i else gather(table_ref, highs[t], hots[t]))
+        across = own_ref[:, cols] + (ends[0] - ends[1])
+        across_ref[:, cols] = across
+        return flows_of(across, cur_ref, chg_ref, cols), highs, hots
+
+    add_up(front, acc_ref)
     put_blocks(acc_ref, out_ref)
 
 
-def own_flow_kernel(flows_ref, term_ref, own_ref, acc_ref):
-    for i, cols in enumerate(tiles()):
+def own_flow_kernel(across_ref, term_ref, cur_ref, chg_ref, own_ref, acc_ref):
+    def front(i):
+        cols = tiles()[i]
         highs, hots = [], []
         for t in range(2):
             node = term_ref[t : t + 1, cols]
             highs.append(node >> SHIFT)
             hots.append(one_hot(node & (LOW - 1)))
-        part = scatter(flows_ref[:, cols], highs, hots)
-        acc_ref[...] = part if i == 0 else acc_ref[...] + part
+        return flows_of(across_ref[:, cols], cur_ref, chg_ref, cols), highs, hots
+
+    add_up(front, acc_ref)
     put_blocks(acc_ref, own_ref)
 
 
@@ -184,11 +218,10 @@
     norm_ref[...] = jnp.sqrt(res_sum)
 
 
-def call(kernel, out_shapes, scratch=(), limit=24, flops=0, types=None):
-    types = types or [F32] * len(out_shapes)
+def call(kernel, out_shapes, scratch=(), limit=24, flops=0):
     return pl.pallas_call(
         kernel,
-        out_shape=[jax.ShapeDtypeStruct(s, t) for s, t in zip(out_shapes, types, strict=True)],
+        out_shape=[jax.ShapeDtypeStruct(s, F32) for s in out_shapes],
         scratch_shapes=list(scratch),
         compiler_params=pltpu.CompilerParams(vmem_limit_bytes=limit * 2**20),
         cost_estimate=pl.CostEstimate(flops=flops, bytes_accessed=2**20, transcendentals=0) if flops else None,
@@ -200,17 +233,14 @@
     border = lax.all_to_all(sent, "dom", 0, 0, tiled=True)
     table_scratch = pltpu.VMEM((2 * HIGHS * ROWS, LOW), BF)
     acc_scratch = pltpu.VMEM((HIGHS * 4 * ROWS, LOW), F32)
+    params = (terminals, elem_current, elem_charge)
     (across,) = call(own_across_kernel, [(ROWS, NE)], [table_scratch], 32, 4 * 10**9)(voltages, terminals)
-    outgoing, flows = call(
-        flow_kernel,
-        [(PARTS, 2 * ROWS, LANES), (4 * ROWS, NE)],
-        [table_scratch, acc_scratch],
-        40,
-        8 * 10**9,
-        [F32, BF],
-    )(border, across, terminals, elem_current, elem_charge)
+    outgoing, across = call(
+        flow_kernel, [(PARTS, 2 * ROWS, LANES), (ROWS, NE)], [table_scratch, acc_scratch], 32, 8 * 10**9
+    )(border, across, *params)
+    own_call = call(own_flow_kernel, [(PARTS, 2 * ROWS, LANES)], [acc_scratch], 32, 6 * 10**9)
+    (own,) = own_call(across, *params)
     incoming = lax.all_to_all(outgoing, "dom", 0, 0, tiled=True)
-    (own,) = call(own_flow_kernel, [(PARTS, 2 * ROWS, LANES)], [acc_scratch], 32, 6 * 10**9)(flows, terminals)
     own = own.at[0].add(jnp.sum(incoming, axis=0))
     flows = lax.all_to_all(own, "freq", 0, 0, tiled=True).reshape(2 * S, LANES)
     table = transform_table()

time: 103 us -> 102 us (level)
  local copies, waits for them, and re-layouts: 3.68 us -> 1.49 us
  Pallas kernels: 17.5 us -> 15.8 us
  waiting for transfers between devices: 8.84 us -> 10.1 us
  other arithmetic: 0.04 us -> 1.08 us
    unnamed x20 -> x16, local copies, waits for them, and re-layouts: 2.23 us -> 0.04 us
    pallas_call x2, Pallas kernels: 12 us -> 10.4 us  [the longest x1 5.89 us: body(): call(flow_kernel, [(PARTS, 2 * ROWS, LANES), (ROWS, NE)], [table_scratch,...]
    all_to_all x1, waiting for transfers between devices: 3.7 us -> 4.96 us  [body(): incoming = lax.all_to_all(outgoing, 'dom', 0, 0, tiled=True)]
    reduce_sum x1, other arithmetic: 0.03 us -> 1.08 us  [body(): own = own.at[0].add(jnp.sum(incoming, axis=0))]
where the time goes in v4:
time: 102 us
  blocking collectives  60.5 us (59%)
  Pallas kernels  15.8 us (15%)
  starting transfers between devices  12 us (12%)
  waiting for transfers between devices  10.1 us (10%)
  local copies, waits for them, and re-layouts  1.49 us (1%)
  other arithmetic  1.08 us (1%)
    all_to_all x1, blocking collectives, body(): flows = lax.all_to_all(own, 'freq', 0, 0, tiled=True).reshape(2 * S, LANES)  28.6 us
    all_to_all x1, blocking collectives, body(): sums = lax.all_to_all(sums, ('dom', 'freq'), 0, 0, tiled=True)  17.3 us
    all_to_all x1, blocking collectives, body(): lax.all_to_all(coef.reshape(PARTS, ROWS, LANES), 'freq', 0, 0, tiled=True)  14.5 us
    all_to_all x1, starting transfers between devices, body(): border = lax.all_to_all(sent, 'dom', 0, 0, tiled=True)  7.72 us
    pallas_call x1, Pallas kernels, body(): call(flow_kernel, [(PARTS, 2 * ROWS, LANES), (ROWS, NE)], [table_scratch,...  5.89 us
    all_to_all x1, waiting for transfers between devices, body(): border = lax.all_to_all(sent, 'dom', 0, 0, tiled=True)  5.14 us
    all_to_all x1, waiting for transfers between devices, body(): incoming = lax.all_to_all(outgoing, 'dom', 0, 0, tiled=True)  4.96 us
    pallas_call x1, Pallas kernels, body(): own, = own_call(across, *params)  4.52 us
  transfers between devices with their start and end apart: 2, of which 2 were waited for; matrix products, arithmetic and copies ran while one was open for 0% of the time, Pallas kernels for 7%

profile of v4, /device:TPU:1, one launch (start us, length us, event | category | flops | bytes accessed | tf_op | source)
XLA Modules:
  0.0 101.7 jit_solution(11160130029007402907)
XLA Ops:
  0.6 0.0 slice-start
  0.6 0.7 slice-done
  1.4 0.7 broadcast_in_dim.2
  2.1 7.7 %all-to-all-start = ((f32[16,32,128]{2,1,0:T(8,128)}), f32[16,32,128]{2,1,0:T(8,128)S(1)}, u32[]{:S(2)}, u32[]{:S(2)}) async-start(f32[16,32,128]{2,1,0:T(8,128)} %broadcast_in_dim.2), calls=%async_computation | async-start | bytes 524288 | tf_op jit(solution)/shard_map/all_to_all | solution.py:233
  9.8 0.0 copy-start.6
  9.8 0.0 copy-start.7
  9.9 2.4 %shard_map.103.own_ref = f32[32,4096]{1,0:T(8,128)S(1)} custom-call(f32[32,2048]{1,0:T(8,128)S(1)} %copy-done.4, s32[2,4096]{1,0:T(2,128)S(1)} %copy-done.5), custom_call_target="tpu_custom_call" | custom-call | flops 4000000000 | bytes 1048576 | tf_op jit(solution)/shard_map/pallas_call | solution.py:237
  12.2 5.1 %all-to-all-done.border_ref = f32[16,32,128]{2,1,0:T(8,128)S(1)} async-done(((f32[16,32,128]{2,1,0:T(8,128)}), f32[16,32,128]{2,1,0:T(8,128)S(1)}, u32[]{:S(2)}, u32[]{:S(2)}) %all-to-all-start) | async-done | bytes 262176 | tf_op jit(solution)/shard_map/all_to_all | solution.py:233
  17.4 0.0 copy-done.7
  17.4 5.9 %shard_map.104 = (f32[16,64,128]{2,1,0:T(8,128)}, f32[32,4096]{1,0:T(8,128)S(1)}) custom-call(f32[16,32,128]{2,1,0:T(8,128)S(1)} %all-to-all-done.border_ref, f32[32,4096]{1,0:T(8,128)S(1)} %shard_map.103.own_ref, s32[2,4096]{1,0:T(2,128)S(1)} %copy-done.5, f32[2,4096]{1,0:T(2,128)S(1)} %copy-done.6, f32[2,4096]{1,0:T(2,128)S(1)} %copy-done.7), custom_call_target="tpu_custom_call" | custom-call | flops 8000000000 | bytes 1048576 | tf_op jit(solution)/shard_map/pallas_call | solution.py:238
  23.2 4.2 %all-to-all-start.1 = ((f32[16,64,128]{2,1,0:T(8,128)}), f32[16,64,128]{2,1,0:T(8,128)}, u32[]{:S(2)}, u32[]{:S(2)}) async-start(f32[16,64,128]{2,1,0:T(8,128)} %get-tuple-element.23), calls=%async_computation.1 | async-start | bytes 1048576 | tf_op jit(solution)/shard_map/all_to_all | solution.py:243
  27.5 0.0 copy-start.1
  27.5 4.5 %shard_map.105 = f32[16,64,128]{2,1,0:T(8,128)S(1)} custom-call(f32[32,4096]{1,0:T(8,128)S(1)} %get-tuple-element.22.across_ref, s32[2,4096]{1,0:T(2,128)S(1)} %copy-done.5, f32[2,4096]{1,0:T(2,128)S(1)} %copy-done.6, f32[2,4096]{1,0:T(2,128)S(1)} %copy-done.7), custom_call_target="tpu_custom_call" | custom-call | flops 6000000000 | bytes 1048576 | tf_op jit(solution)/shard_map/pallas_call | solution.py:242
  32.0 0.0 copy-start
  32.1 5.0 %all-to-all-done.1 = f32[16,64,128]{2,1,0:T(8,128)} async-done(((f32[16,64,128]{2,1,0:T(8,128)}), f32[16,64,128]{2,1,0:T(8,128)}, u32[]{:S(2)}, u32[]{:S(2)}) %all-to-all-start.1) | async-done | bytes 524320 | tf_op jit(solution)/shard_map/all_to_all | solution.py:243
  37.0 1.1 %reduce_sum.9 = f32[64,128]{1,0:T(8,128)S(1)} reduce(f32[16,64,128]{2,1,0:T(8,128)} %all-to-all-done.1, f32[]{:T(128)} %constant.31.clone.1), dimensions={0}, to_apply=%region_0.0 | reduce | flops 122880 | bytes 557060 | tf_op jit(solution)/shard_map/reduce_sum | solution.py:244
  38.1 28.6 %all_to_all.31 = f32[16,64,128]{2,1,0:T(8,128)S(1)} all-to-all(f32[16,64,128]{2,1,0:T(8,128)S(1)} %fusion), channel_id=1, replica_groups=mesh['dom'=16,'freq'=16] {'freq'}, dimensions={0} | all-to-all | bytes 1048576 | tf_op jit(solution)/shard_map/all_to_all | solution.py:245
  66.7 1.0 shard_map.106
  67.7 0.0 copy-start.2
  67.7 14.5 %all_to_all.32.coef_ref = f32[16,32,128]{2,1,0:T(8,128)S(1)} all-to-all(f32[16,32,128]{2,1,0:T(8,128)S(1)} %bitcast.11), channel_id=1, replica_groups=mesh['dom'=16,'freq'=16] {'freq'}, dimensions={0} | all-to-all | bytes 524288 | tf_op jit(solution)/shard_map/all_to_all | solution.py:250
  82.3 0.0 copy-done.2
  82.3 1.2 %shard_map.107 = (f32[32,2048]{1,0:T(8,128)}, f32[32,2048]{1,0:T(8,128)S(1)}, f32[256,128]{1,0:T(8,128)S(1)}) custom-call(f32[16,32,128]{2,1,0:T(8,128)S(1)} %all_to_all.32.coef_ref, f32[32,2048]{1,0:T(8,128)S(1)} %copy-done.3, f32[32,2,2048]{2,1,0:T(2,128)S(1)} %bitcast.13), custom_call_target="tpu_custom_call" | custom-call | tf_op jit(solution)/shard_map/pallas_call | solution.py:251
  83.5 17.3 %all_to_all.33 = f32[256,1,128]{2,1,0:T(1,128)S(1)} all-to-all(f32[256,1,128]{2,1,0:T(1,128)S(1)} %bitcast.14), channel_id=1, replica_groups=mesh['dom'=16,'freq'=16] {'dom','freq'}, dimensions={0} | all-to-all | bytes 262144 | tf_op jit(solution)/shard_map/all_to_all | solution.py:254
  100.8 0.9 shard_map.108
  (10 shorter events, 0.0 us)
Async XLA Ops:
  0.6 0.7 slice-start
  2.1 7.7 %copy-start.4 = (f32[32,2048]{1,0:T(8,128)S(1)}, f32[32,2048]{1,0:T(8,128)}, u32[]{:S(2)}) copy-start(f32[32,2048]{1,0:T(8,128)} %volt_ref.1) | copy-start | bytes 786436
  2.1 7.7 %copy-start.5 = (s32[2,4096]{1,0:T(2,128)S(1)}, s32[2,4096]{1,0:T(2,128)}, u32[]{:S(2)}) copy-start(s32[2,4096]{1,0:T(2,128)} %term_ref.5) | copy-start | bytes 98308
  2.1 15.3 %all-to-all-start = ((f32[16,32,128]{2,1,0:T(8,128)}), f32[16,32,128]{2,1,0:T(8,128)S(1)}, u32[]{:S(2)}, u32[]{:S(2)}) async-start(f32[16,32,128]{2,1,0:T(8,128)} %broadcast_in_dim.2), calls=%async_computation | async-start | bytes 524288 | tf_op jit(solution)/shard_map/all_to_all | solution.py:233
  9.8 7.5 %copy-start.6 = (f32[2,4096]{1,0:T(2,128)S(1)}, f32[2,4096]{1,0:T(2,128)}, u32[]{:S(2)}) copy-start(f32[2,4096]{1,0:T(2,128)} %cur_ref.3) | copy-start | bytes 98308
  9.8 7.5 %copy-start.7 = (f32[2,4096]{1,0:T(2,128)S(1)}, f32[2,4096]{1,0:T(2,128)}, u32[]{:S(2)}) copy-start(f32[2,4096]{1,0:T(2,128)} %chg_ref.3) | copy-start | bytes 98308
  23.2 13.8 %all-to-all-start.1 = ((f32[16,64,128]{2,1,0:T(8,128)}), f32[16,64,128]{2,1,0:T(8,128)}, u32[]{:S(2)}, u32[]{:S(2)}) async-start(f32[16,64,128]{2,1,0:T(8,128)} %get-tuple-element.23), calls=%async_computation.1 | async-start | bytes 1048576 | tf_op jit(solution)/shard_map/all_to_all | solution.py:243
  27.5 39.2 %copy-start.1 = (bf16[512,1024]{1,0:T(8,128)(2,1)S(1)}, bf16[512,1024]{1,0:T(8,128)(2,1)}, u32[]{:S(2)}) copy-start(bf16[512,1024]{1,0:T(8,128)(2,1)} %constant.33.clone.high_ref) | copy-start | bytes 3145732
  32.0 34.7 %copy-start = (bf16[512,1024]{1,0:T(8,128)(2,1)S(1)}, bf16[512,1024]{1,0:T(8,128)(2,1)}, u32[]{:S(2)}) copy-start(bf16[512,1024]{1,0:T(8,128)(2,1)} %constant.34.clone.low_ref) | copy-start | bytes 3145732
  66.7 15.5 %copy-start.3 = (f32[32,2048]{1,0:T(8,128)S(1)}, f32[32,2048]{1,0:T(8,128)}, u32[]{:S(2)}) copy-start(f32[32,2048]{1,0:T(8,128)} %src_ref.1) | copy-start | bytes 786436
  67.7 14.6 %copy-start.2 = (f32[16,2,2,2048]{3,2,1,0:T(2,128)S(1)}, f32[16,2,2,2048]{3,2,1,0:T(2,128)}, u32[]{:S(2)}) copy-start(f32[16,2,2,2048]{3,2,1,0:T(2,128)} %param.15) | copy-start | bytes 1572868

commit v5 on v4

--- a/solution.py
+++ b/solution.py
@@ -1,4 +1,3 @@
-import functools
 import math
 
 import jax
@@ -181,10 +180,20 @@
     put_blocks(acc_ref, own_ref)
 
 
+def border_kernel(own_ref, incoming_ref, out_ref):
+    total = own_ref[0]
+    for p in range(PARTS):
+        total = total + incoming_ref[p]
+    out_ref[0] = total
+    for k in range(1, PARTS):
+        out_ref[k] = own_ref[k]
+
+
 def transform_kernel(flow_ref, high_ref, low_ref, out_ref):
     hi, lo = split(flow_ref[...])
-    dot = functools.partial(jnp.dot, preferred_element_type=F32)
-    out_ref[...] = dot(high_ref[...], hi) + (dot(high_ref[...], lo) + dot(low_ref[...], hi))
+    both = jnp.dot(high_ref[...], jnp.concatenate([hi, lo], axis=1), preferred_element_type=F32)
+    rest = jnp.dot(low_ref[...], hi, preferred_element_type=F32)
+    out_ref[...] = both[:, :LANES] + (both[:, LANES:] + rest)
 
 
 def step_kernel(coef_ref, src_ref, jac_ref, res_ref, raw_ref, sums_ref):
@@ -241,7 +250,14 @@
     own_call = call(own_flow_kernel, [(PARTS, 2 * ROWS, LANES)], [acc_scratch], 32, 6 * 10**9)
     (own,) = own_call(across, *params)
     incoming = lax.all_to_all(outgoing, "dom", 0, 0, tiled=True)
-    own = own.at[0].add(jnp.sum(incoming, axis=0))
+    own = pl.pallas_call(
+        border_kernel,
+        out_shape=jax.ShapeDtypeStruct(own.shape, F32),
+
+        in_specs=[pl.BlockSpec(memory_space=pltpu.VMEM)] * 2,
+        out_specs=pl.BlockSpec(memory_space=pltpu.VMEM),
+        compiler_params=pltpu.CompilerParams(vmem_limit_bytes=8 * 2**20),
+    )(own, incoming)
     flows = lax.all_to_all(own, "freq", 0, 0, tiled=True).reshape(2 * S, LANES)
     table = transform_table()
     high = table.astype(ml_dtypes.bfloat16)

time: 102 us -> 100 us (0.980)
  other arithmetic: 1.08 us -> 0 us
    reduce_sum x1 -> x0, other arithmetic: 1.08 us -> none  [body(): own = own.at[0].add(jnp.sum(incoming, axis=0))]
where the time goes in v5:
time: 100 us; the launch traced here: 99.7 us
  blocking collectives  60.5 us (60%)
  Pallas kernels  15.6 us (16%)
  starting transfers between devices  11.3 us (11%)
  waiting for transfers between devices  10.1 us (10%)
  local copies, waits for them, and re-layouts  1.49 us (1%)
    all_to_all x1, blocking collectives, body(): flows = lax.all_to_all(own, 'freq', 0, 0, tiled=True).reshape(2 * S, LANES)  28.6 us
    all_to_all x1, blocking collectives, body(): sums = lax.all_to_all(sums, ('dom', 'freq'), 0, 0, tiled=True)  17.3 us
    all_to_all x1, blocking collectives, body(): lax.all_to_all(coef.reshape(PARTS, ROWS, LANES), 'freq', 0, 0, tiled=True)  14.5 us
    all_to_all x1, starting transfers between devices, body(): border = lax.all_to_all(sent, 'dom', 0, 0, tiled=True)  7.72 us
    pallas_call x1, Pallas kernels, body(): call(flow_kernel, [(PARTS, 2 * ROWS, LANES), (ROWS, NE)], [table_scratch,...  5.88 us
    all_to_all x1, waiting for transfers between devices, body(): border = lax.all_to_all(sent, 'dom', 0, 0, tiled=True)  5.14 us
    all_to_all x1, waiting for transfers between devices, body(): incoming = lax.all_to_all(outgoing, 'dom', 0, 0, tiled=True)  4.92 us
    pallas_call x1, Pallas kernels, body(): own, = own_call(across, *params)  4.52 us
  transfers between devices with their start and end apart: 2, of which 2 were waited for; matrix products, arithmetic and copies ran while one was open for 0% of the time, Pallas kernels for 7%

profile of v5, /device:TPU:1, one launch (start us, length us, event | category | flops | bytes accessed | tf_op | source)
XLA Modules:
  0.0 99.7 jit_solution(16092417018893594489)
XLA Ops:
  0.6 0.0 slice-start
  0.6 0.7 slice-done
  1.4 0.7 broadcast_in_dim.2
  2.1 7.7 %all-to-all-start = ((f32[16,32,128]{2,1,0:T(8,128)}), f32[16,32,128]{2,1,0:T(8,128)S(1)}, u32[]{:S(2)}, u32[]{:S(2)}) async-start(f32[16,32,128]{2,1,0:T(8,128)} %broadcast_in_dim.2), calls=%async_computation | async-start | bytes 524288 | tf_op jit(solution)/shard_map/all_to_all | solution.py:242
  9.8 0.0 copy-done.4
  9.8 0.0 copy-start.6
  9.8 0.0 copy-start.7
  9.9 2.4 %shard_map.103.own_ref = f32[32,4096]{1,0:T(8,128)S(1)} custom-call(f32[32,2048]{1,0:T(8,128)S(1)} %copy-done.4, s32[2,4096]{1,0:T(2,128)S(1)} %copy-done.5), custom_call_target="tpu_custom_call" | custom-call | flops 4000000000 | bytes 1048576 | tf_op jit(solution)/shard_map/pallas_call | solution.py:246
  12.2 5.1 %all-to-all-done.border_ref = f32[16,32,128]{2,1,0:T(8,128)S(1)} async-done(((f32[16,32,128]{2,1,0:T(8,128)}), f32[16,32,128]{2,1,0:T(8,128)S(1)}, u32[]{:S(2)}, u32[]{:S(2)}) %all-to-all-start) | async-done | bytes 262176 | tf_op jit(solution)/shard_map/all_to_all | solution.py:242
  17.4 5.9 %shard_map.104 = (f32[16,64,128]{2,1,0:T(8,128)}, f32[32,4096]{1,0:T(8,128)S(1)}) custom-call(f32[16,32,128]{2,1,0:T(8,128)S(1)} %all-to-all-done.border_ref, f32[32,4096]{1,0:T(8,128)S(1)} %shard_map.103.own_ref, s32[2,4096]{1,0:T(2,128)S(1)} %copy-done.5, f32[2,4096]{1,0:T(2,128)S(1)} %copy-done.6, f32[2,4096]{1,0:T(2,128)S(1)} %copy-done.7), custom_call_target="tpu_custom_call" | custom-call | flops 8000000000 | bytes 1048576 | tf_op jit(solution)/shard_map/pallas_call | solution.py:247
  23.2 3.6 %all-to-all-start.1 = ((f32[16,64,128]{2,1,0:T(8,128)}), f32[16,64,128]{2,1,0:T(8,128)S(1)}, u32[]{:S(2)}, u32[]{:S(2)}) async-start(f32[16,64,128]{2,1,0:T(8,128)} %get-tuple-element.11), calls=%async_computation.1 | async-start | bytes 1048576 | tf_op jit(solution)/shard_map/all_to_all | solution.py:252
  26.8 4.5 %shard_map.105.own_ref = f32[16,64,128]{2,1,0:T(8,128)S(1)} custom-call(f32[32,4096]{1,0:T(8,128)S(1)} %get-tuple-element.10.across_ref, s32[2,4096]{1,0:T(2,128)S(1)} %copy-done.5, f32[2,4096]{1,0:T(2,128)S(1)} %copy-done.6, f32[2,4096]{1,0:T(2,128)S(1)} %copy-done.7), custom_call_target="tpu_custom_call" | custom-call | flops 6000000000 | bytes 1048576 | tf_op jit(solution)/shard_map/pallas_call | solution.py:251
  31.3 0.0 copy-start
  31.4 0.0 copy-start.1
  31.4 4.9 %all-to-all-done.1.incoming_ref = f32[16,64,128]{2,1,0:T(8,128)S(1)} async-done(((f32[16,64,128]{2,1,0:T(8,128)}), f32[16,64,128]{2,1,0:T(8,128)S(1)}, u32[]{:S(2)}, u32[]{:S(2)}) %all-to-all-start.1) | async-done | bytes 524320 | tf_op jit(solution)/shard_map/all_to_all | solution.py:252
  36.3 0.1 shard_map.106
  36.3 28.6 %all_to_all.31 = f32[16,64,128]{2,1,0:T(8,128)S(1)} all-to-all(f32[16,64,128]{2,1,0:T(8,128)S(1)} %shard_map.106), channel_id=1, replica_groups=mesh['dom'=16,'freq'=16] {'freq'}, dimensions={0} | all-to-all | bytes 1048576 | tf_op jit(solution)/shard_map/all_to_all | solution.py:261
  65.0 0.7 shard_map.107
  65.7 0.0 copy-start.2
  65.7 14.5 %all_to_all.32.coef_ref = f32[16,32,128]{2,1,0:T(8,128)S(1)} all-to-all(f32[16,32,128]{2,1,0:T(8,128)S(1)} %bitcast.9), channel_id=1, replica_groups=mesh['dom'=16,'freq'=16] {'freq'}, dimensions={0} | all-to-all | bytes 524288 | tf_op jit(solution)/shard_map/all_to_all | solution.py:266
  80.2 0.0 copy-done.2
  80.2 1.2 %shard_map.108 = (f32[32,2048]{1,0:T(8,128)}, f32[32,2048]{1,0:T(8,128)S(1)}, f32[256,128]{1,0:T(8,128)S(1)}) custom-call(f32[16,32,128]{2,1,0:T(8,128)S(1)} %all_to_all.32.coef_ref, f32[32,2048]{1,0:T(8,128)S(1)} %copy-done.3, f32[32,2,2048]{2,1,0:T(2,128)S(1)} %bitcast.11), custom_call_target="tpu_custom_call" | custom-call | tf_op jit(solution)/shard_map/pallas_call | solution.py:267
  81.5 17.3 %all_to_all.33 = f32[256,1,128]{2,1,0:T(1,128)S(1)} all-to-all(f32[256,1,128]{2,1,0:T(1,128)S(1)} %bitcast.12), channel_id=1, replica_groups=mesh['dom'=16,'freq'=16] {'dom','freq'}, dimensions={0} | all-to-all | bytes 262144 | tf_op jit(solution)/shard_map/all_to_all | solution.py:270
  98.8 0.9 shard_map.109
  (9 shorter events, 0.0 us)
Async XLA Ops:
  0.6 0.7 slice-start
  2.1 7.7 %copy-start.4 = (f32[32,2048]{1,0:T(8,128)S(1)}, f32[32,2048]{1,0:T(8,128)}, u32[]{:S(2)}) copy-start(f32[32,2048]{1,0:T(8,128)} %volt_ref.1) | copy-start | bytes 786436
  2.1 7.7 %copy-start.5 = (s32[2,4096]{1,0:T(2,128)S(1)}, s32[2,4096]{1,0:T(2,128)}, u32[]{:S(2)}) copy-start(s32[2,4096]{1,0:T(2,128)} %term_ref.5) | copy-start | bytes 98308
  2.1 15.3 %all-to-all-start = ((f32[16,32,128]{2,1,0:T(8,128)}), f32[16,32,128]{2,1,0:T(8,128)S(1)}, u32[]{:S(2)}, u32[]{:S(2)}) async-start(f32[16,32,128]{2,1,0:T(8,128)} %broadcast_in_dim.2), calls=%async_computation | async-start | bytes 524288 | tf_op jit(solution)/shard_map/all_to_all | solution.py:242
  9.8 7.5 %copy-start.6 = (f32[2,4096]{1,0:T(2,128)S(1)}, f32[2,4096]{1,0:T(2,128)}, u32[]{:S(2)}) copy-start(f32[2,4096]{1,0:T(2,128)} %cur_ref.3) | copy-start | bytes 98308
  9.8 7.5 %copy-start.7 = (f32[2,4096]{1,0:T(2,128)S(1)}, f32[2,4096]{1,0:T(2,128)}, u32[]{:S(2)}) copy-start(f32[2,4096]{1,0:T(2,128)} %chg_ref.3) | copy-start | bytes 98308
  23.2 13.0 %all-to-all-start.1 = ((f32[16,64,128]{2,1,0:T(8,128)}), f32[16,64,128]{2,1,0:T(8,128)S(1)}, u32[]{:S(2)}, u32[]{:S(2)}) async-start(f32[16,64,128]{2,1,0:T(8,128)} %get-tuple-element.11), calls=%async_computation.1 | async-start | bytes 1048576 | tf_op jit(solution)/shard_map/all_to_all | solution.py:252
  31.3 33.6 %copy-start = (bf16[512,1024]{1,0:T(8,128)(2,1)S(1)}, bf16[512,1024]{1,0:T(8,128)(2,1)}, u32[]{:S(2)}) copy-start(bf16[512,1024]{1,0:T(8,128)(2,1)} %constant.5.clone.low_ref) | copy-start | bytes 3145732
  31.4 33.6 %copy-start.1 = (bf16[512,1024]{1,0:T(8,128)(2,1)S(1)}, bf16[512,1024]{1,0:T(8,128)(2,1)}, u32[]{:S(2)}) copy-start(bf16[512,1024]{1,0:T(8,128)(2,1)} %constant.4.clone.high_ref) | copy-start | bytes 3145732
  65.0 15.3 %copy-start.3 = (f32[32,2048]{1,0:T(8,128)S(1)}, f32[32,2048]{1,0:T(8,128)}, u32[]{:S(2)}) copy-start(f32[32,2048]{1,0:T(8,128)} %src_ref.1) | copy-start | bytes 786436
  65.7 14.6 %copy-start.2 = (f32[16,2,2,2048]{3,2,1,0:T(2,128)S(1)}, f32[16,2,2,2048]{3,2,1,0:T(2,128)}, u32[]{:S(2)}) copy-start(f32[16,2,2,2048]{3,2,1,0:T(2,128)} %param.13) | copy-start | bytes 1572868

commit v6 on v5

--- a/solution.py
+++ b/solution.py
@@ -217,7 +217,8 @@
     sums_ref[...] = jnp.broadcast_to(row, sums_ref.shape)
 
 
-def scale_kernel(raw_ref, sums_ref, out_ref, norm_ref):
+def scale_kernel(res_ref, raw_ref, sums_ref, res_out_ref, out_ref, norm_ref):
+    res_out_ref[...] = res_ref[...]
     row = jnp.sum(sums_ref[...], axis=0, keepdims=True)
     half = lax.broadcasted_iota(jnp.int32, (1, LANES), 1) < LANES // 2
     raw_sum = jnp.sum(jnp.where(half, row, 0.0), axis=1, keepdims=True)
@@ -253,7 +254,6 @@
     own = pl.pallas_call(
         border_kernel,
         out_shape=jax.ShapeDtypeStruct(own.shape, F32),
-
         in_specs=[pl.BlockSpec(memory_space=pltpu.VMEM)] * 2,
         out_specs=pl.BlockSpec(memory_space=pltpu.VMEM),
         compiler_params=pltpu.CompilerParams(vmem_limit_bytes=8 * 2**20),
@@ -262,13 +262,15 @@
     table = transform_table()
     high = table.astype(ml_dtypes.bfloat16)
     low = (table - high.astype(np.float64)).astype(ml_dtypes.bfloat16)
-    (coef,) = call(transform_kernel, [(S, LANES)], )(flows, jnp.asarray(high), jnp.asarray(low))
+    (coef,) = call(transform_kernel, [(S, LANES)], (), 12)(flows, jnp.asarray(high), jnp.asarray(low))
     coef = lax.all_to_all(coef.reshape(PARTS, ROWS, LANES), "freq", 0, 0, tiled=True)
-    residual, raw, sums = call(step_kernel, [(ROWS, NPD), (ROWS, NPD), (256, LANES)], )(
+    residual, raw, sums = call(step_kernel, [(ROWS, NPD), (ROWS, NPD), (256, LANES)], (), 12)(
         coef, sources, jacobi.reshape(ROWS, 2, NPD)
     )
     sums = lax.all_to_all(sums, ("dom", "freq"), 0, 0, tiled=True)
-    newton_step, norm = call(scale_kernel, [(ROWS, NPD), (1, 1)], )(raw, sums)
+    residual, newton_step, norm = call(scale_kernel, [(ROWS, NPD), (ROWS, NPD), (1, 1)], (), 12)(
+        residual, raw, sums
+    )
     return residual, newton_step, norm.reshape(())
 
 

time: 100 us -> 99.6 us (level)
  no operation moved by 1% of the time
where the time goes in v6:
time: 99.6 us; the launch traced here: 99.1 us
  blocking collectives  60.5 us (61%)
  Pallas kernels  15.1 us (15%)
  starting transfers between devices  11.3 us (11%)
  waiting for transfers between devices  10.1 us (10%)
  local copies, waits for them, and re-layouts  1.49 us (1%)
    all_to_all x1, blocking collectives, body(): flows = lax.all_to_all(own, 'freq', 0, 0, tiled=True).reshape(2 * S, LANES)  28.6 us
    all_to_all x1, blocking collectives, body(): sums = lax.all_to_all(sums, ('dom', 'freq'), 0, 0, tiled=True)  17.3 us
    all_to_all x1, blocking collectives, body(): lax.all_to_all(coef.reshape(PARTS, ROWS, LANES), 'freq', 0, 0, tiled=True)  14.5 us
    all_to_all x1, starting transfers between devices, body(): border = lax.all_to_all(sent, 'dom', 0, 0, tiled=True)  7.72 us
    pallas_call x1, Pallas kernels, body(): call(flow_kernel, [(PARTS, 2 * ROWS, LANES), (ROWS, NE)], [table_scratch,...  5.88 us
    all_to_all x1, waiting for transfers between devices, body(): border = lax.all_to_all(sent, 'dom', 0, 0, tiled=True)  5.14 us
    all_to_all x1, waiting for transfers between devices, body(): incoming = lax.all_to_all(outgoing, 'dom', 0, 0, tiled=True)  4.92 us
    pallas_call x1, Pallas kernels, body(): own, = own_call(across, *params)  4.52 us
  transfers between devices with their start and end apart: 2, of which 2 were waited for; matrix products, arithmetic and copies ran while one was open for 0% of the time, Pallas kernels for 7%

profile of v6, /device:TPU:1, one launch (start us, length us, event | category | flops | bytes accessed | tf_op | source)
XLA Modules:
  0.0 99.1 jit_solution(12944729536345131595)
XLA Ops:
  0.6 0.0 slice-start
  0.6 0.7 slice-done
  1.4 0.7 broadcast_in_dim.2
  2.1 7.7 %all-to-all-start = ((f32[16,32,128]{2,1,0:T(8,128)}), f32[16,32,128]{2,1,0:T(8,128)S(1)}, u32[]{:S(2)}, u32[]{:S(2)}) async-start(f32[16,32,128]{2,1,0:T(8,128)} %broadcast_in_dim.2), calls=%async_computation | async-start | bytes 524288 | tf_op jit(solution)/shard_map/all_to_all | solution.py:243
  9.8 0.0 copy-start.6
  9.8 0.0 copy-start.7
  9.9 2.4 %shard_map.103.own_ref = f32[32,4096]{1,0:T(8,128)S(1)} custom-call(f32[32,2048]{1,0:T(8,128)S(1)} %copy-done.4, s32[2,4096]{1,0:T(2,128)S(1)} %copy-done.5), custom_call_target="tpu_custom_call" | custom-call | flops 4000000000 | bytes 1048576 | tf_op jit(solution)/shard_map/pallas_call | solution.py:247
  12.2 5.1 %all-to-all-done.border_ref = f32[16,32,128]{2,1,0:T(8,128)S(1)} async-done(((f32[16,32,128]{2,1,0:T(8,128)}), f32[16,32,128]{2,1,0:T(8,128)S(1)}, u32[]{:S(2)}, u32[]{:S(2)}) %all-to-all-start) | async-done | bytes 262176 | tf_op jit(solution)/shard_map/all_to_all | solution.py:243
  17.4 0.0 copy-done.7
  17.4 5.9 %shard_map.104 = (f32[16,64,128]{2,1,0:T(8,128)}, f32[32,4096]{1,0:T(8,128)S(1)}) custom-call(f32[16,32,128]{2,1,0:T(8,128)S(1)} %all-to-all-done.border_ref, f32[32,4096]{1,0:T(8,128)S(1)} %shard_map.103.own_ref, s32[2,4096]{1,0:T(2,128)S(1)} %copy-done.5, f32[2,4096]{1,0:T(2,128)S(1)} %copy-done.6, f32[2,4096]{1,0:T(2,128)S(1)} %copy-done.7), custom_call_target="tpu_custom_call" | custom-call | flops 8000000000 | bytes 1048576 | tf_op jit(solution)/shard_map/pallas_call | solution.py:248
  23.2 3.6 %all-to-all-start.1 = ((f32[16,64,128]{2,1,0:T(8,128)}), f32[16,64,128]{2,1,0:T(8,128)S(1)}, u32[]{:S(2)}, u32[]{:S(2)}) async-start(f32[16,64,128]{2,1,0:T(8,128)} %get-tuple-element.12), calls=%async_computation.1 | async-start | bytes 1048576 | tf_op jit(solution)/shard_map/all_to_all | solution.py:253
  26.8 4.5 %shard_map.105.own_ref = f32[16,64,128]{2,1,0:T(8,128)S(1)} custom-call(f32[32,4096]{1,0:T(8,128)S(1)} %get-tuple-element.11.across_ref, s32[2,4096]{1,0:T(2,128)S(1)} %copy-done.5, f32[2,4096]{1,0:T(2,128)S(1)} %copy-done.6, f32[2,4096]{1,0:T(2,128)S(1)} %copy-done.7), custom_call_target="tpu_custom_call" | custom-call | flops 6000000000 | bytes 1048576 | tf_op jit(solution)/shard_map/pallas_call | solution.py:252
  31.3 0.0 copy-start
  31.4 0.0 copy-start.1
  31.4 4.9 %all-to-all-done.1.incoming_ref = f32[16,64,128]{2,1,0:T(8,128)S(1)} async-done(((f32[16,64,128]{2,1,0:T(8,128)}), f32[16,64,128]{2,1,0:T(8,128)S(1)}, u32[]{:S(2)}, u32[]{:S(2)}) %all-to-all-start.1) | async-done | bytes 524320 | tf_op jit(solution)/shard_map/all_to_all | solution.py:253
  36.3 0.1 shard_map.106
  36.3 28.6 %all_to_all.31 = f32[16,64,128]{2,1,0:T(8,128)S(1)} all-to-all(f32[16,64,128]{2,1,0:T(8,128)S(1)} %shard_map.106), channel_id=1, replica_groups=mesh['dom'=16,'freq'=16] {'freq'}, dimensions={0} | all-to-all | bytes 1048576 | tf_op jit(solution)/shard_map/all_to_all | solution.py:261
  65.0 0.0 copy-done
  65.0 0.7 shard_map.107
  65.7 0.0 copy-start.2
  65.7 14.5 %all_to_all.32.coef_ref = f32[16,32,128]{2,1,0:T(8,128)S(1)} all-to-all(f32[16,32,128]{2,1,0:T(8,128)S(1)} %bitcast.9), channel_id=1, replica_groups=mesh['dom'=16,'freq'=16] {'freq'}, dimensions={0} | all-to-all | bytes 524288 | tf_op jit(solution)/shard_map/all_to_all | solution.py:266
  80.2 0.7 shard_map.108
  80.9 17.3 %all_to_all.33 = f32[256,1,128]{2,1,0:T(1,128)S(1)} all-to-all(f32[256,1,128]{2,1,0:T(1,128)S(1)} %bitcast.12), channel_id=1, replica_groups=mesh['dom'=16,'freq'=16] {'dom','freq'}, dimensions={0} | all-to-all | bytes 262144 | tf_op jit(solution)/shard_map/all_to_all | solution.py:270
  98.3 0.9 shard_map.109
  (9 shorter events, 0.0 us)
Async XLA Ops:
  0.6 0.7 slice-start
  2.1 7.7 %copy-start.4 = (f32[32,2048]{1,0:T(8,128)S(1)}, f32[32,2048]{1,0:T(8,128)}, u32[]{:S(2)}) copy-start(f32[32,2048]{1,0:T(8,128)} %volt_ref.1) | copy-start | bytes 786436
  2.1 7.7 %copy-start.5 = (s32[2,4096]{1,0:T(2,128)S(1)}, s32[2,4096]{1,0:T(2,128)}, u32[]{:S(2)}) copy-start(s32[2,4096]{1,0:T(2,128)} %term_ref.5) | copy-start | bytes 98308
  2.1 15.3 %all-to-all-start = ((f32[16,32,128]{2,1,0:T(8,128)}), f32[16,32,128]{2,1,0:T(8,128)S(1)}, u32[]{:S(2)}, u32[]{:S(2)}) async-start(f32[16,32,128]{2,1,0:T(8,128)} %broadcast_in_dim.2), calls=%async_computation | async-start | bytes 524288 | tf_op jit(solution)/shard_map/all_to_all | solution.py:243
  9.8 7.5 %copy-start.6 = (f32[2,4096]{1,0:T(2,128)S(1)}, f32[2,4096]{1,0:T(2,128)}, u32[]{:S(2)}) copy-start(f32[2,4096]{1,0:T(2,128)} %cur_ref.3) | copy-start | bytes 98308
  9.8 7.5 %copy-start.7 = (f32[2,4096]{1,0:T(2,128)S(1)}, f32[2,4096]{1,0:T(2,128)}, u32[]{:S(2)}) copy-start(f32[2,4096]{1,0:T(2,128)} %chg_ref.3) | copy-start | bytes 98308
  23.2 13.0 %all-to-all-start.1 = ((f32[16,64,128]{2,1,0:T(8,128)}), f32[16,64,128]{2,1,0:T(8,128)S(1)}, u32[]{:S(2)}, u32[]{:S(2)}) async-start(f32[16,64,128]{2,1,0:T(8,128)} %get-tuple-element.12), calls=%async_computation.1 | async-start | bytes 1048576 | tf_op jit(solution)/shard_map/all_to_all | solution.py:253
  31.3 33.6 %copy-start = (bf16[512,1024]{1,0:T(8,128)(2,1)S(1)}, bf16[512,1024]{1,0:T(8,128)(2,1)}, u32[]{:S(2)}) copy-start(bf16[512,1024]{1,0:T(8,128)(2,1)} %constant.5.clone.low_ref) | copy-start | bytes 3145732
  31.4 33.6 %copy-start.1 = (bf16[512,1024]{1,0:T(8,128)(2,1)S(1)}, bf16[512,1024]{1,0:T(8,128)(2,1)}, u32[]{:S(2)}) copy-start(bf16[512,1024]{1,0:T(8,128)(2,1)} %constant.4.clone.high_ref) | copy-start | bytes 3145732
  65.0 15.3 %copy-start.3 = (f32[32,2048]{1,0:T(8,128)S(1)}, f32[32,2048]{1,0:T(8,128)}, u32[]{:S(2)}) copy-start(f32[32,2048]{1,0:T(8,128)} %src_ref.1) | copy-start | bytes 786436
  65.7 14.6 %copy-start.2 = (f32[16,2,2,2048]{3,2,1,0:T(2,128)S(1)}, f32[16,2,2,2048]{3,2,1,0:T(2,128)}, u32[]{:S(2)}) copy-start(f32[16,2,2,2048]{3,2,1,0:T(2,128)} %param.13) | copy-start | bytes 1572868

commit v7 on v6

--- a/solution.py
+++ b/solution.py
@@ -21,6 +21,7 @@
 HIGHS = NPD // LOW
 PER = LOW // LANES
 TILE = 1024
+FLOW_TILES = (768, 896, 896, 896, 640)
 
 trust_radius = 2.0
 BF = jnp.bfloat16
@@ -114,8 +115,9 @@
             out_ref[a * PER + k] = total[:, k * LANES : (k + 1) * LANES]
 
 
-def tiles():
-    return [slice(first, first + TILE) for first in range(0, NE, TILE)]
+def tiles(sizes=(TILE,) * (NE // TILE)):
+    ends = [sum(sizes[: i + 1]) for i in range(len(sizes))]
+    return [slice(end - size, end) for size, end in zip(sizes, ends, strict=True)]
 
 
 def own_across_kernel(volt_ref, term_ref, across_ref, table_ref):
@@ -134,8 +136,7 @@
     return jnp.concatenate(split(jnp.concatenate([current, charge], axis=0)), axis=0)
 
 
-def add_up(front, acc_ref):
-    count = NE // TILE
+def add_up(front, count, acc_ref):
     now = front(0)
     for i in range(count):
         later = front(i + 1) if i + 1 < count else None
@@ -151,7 +152,7 @@
     fill_table(blocks, table_ref)
 
     def front(i):
-        cols = tiles()[i]
+        cols = tiles(FLOW_TILES)[i]
         highs, hots, ends = [], [], []
         for t in range(2):
             node = term_ref[t : t + 1, cols]
@@ -162,7 +163,7 @@
         across_ref[:, cols] = across
         return flows_of(across, cur_ref, chg_ref, cols), highs, hots
 
-    add_up(front, acc_ref)
+    add_up(front, len(FLOW_TILES), acc_ref)
     put_blocks(acc_ref, out_ref)
 
 
@@ -176,7 +177,7 @@
             hots.append(one_hot(node & (LOW - 1)))
         return flows_of(across_ref[:, cols], cur_ref, chg_ref, cols), highs, hots
 
-    add_up(front, acc_ref)
+    add_up(front, NE // TILE, acc_ref)
     put_blocks(acc_ref, own_ref)
 
 

time: 99.6 us -> 99.5 us (level)
  no operation moved by 1% of the time
where the time goes in v7:
time: 99.5 us; the launch traced here: 99 us
  blocking collectives  60.5 us (61%)
  Pallas kernels  15 us (15%)
  starting transfers between devices  11.3 us (11%)
  waiting for transfers between devices  10.1 us (10%)
  local copies, waits for them, and re-layouts  1.49 us (1%)
    all_to_all x1, blocking collectives, body(): flows = lax.all_to_all(own, 'freq', 0, 0, tiled=True).reshape(2 * S, LANES)  28.6 us
    all_to_all x1, blocking collectives, body(): sums = lax.all_to_all(sums, ('dom', 'freq'), 0, 0, tiled=True)  17.3 us
    all_to_all x1, blocking collectives, body(): lax.all_to_all(coef.reshape(PARTS, ROWS, LANES), 'freq', 0, 0, tiled=True)  14.5 us
    all_to_all x1, starting transfers between devices, body(): border = lax.all_to_all(sent, 'dom', 0, 0, tiled=True)  7.72 us
    pallas_call x1, Pallas kernels, body(): call(flow_kernel, [(PARTS, 2 * ROWS, LANES), (ROWS, NE)], [table_scratch,...  5.8 us
    all_to_all x1, waiting for transfers between devices, body(): border = lax.all_to_all(sent, 'dom', 0, 0, tiled=True)  5.14 us
    all_to_all x1, waiting for transfers between devices, body(): incoming = lax.all_to_all(outgoing, 'dom', 0, 0, tiled=True)  4.92 us
    pallas_call x1, Pallas kernels, body(): own, = own_call(across, *params)  4.52 us
  transfers between devices with their start and end apart: 2, of which 2 were waited for; matrix products, arithmetic and copies ran while one was open for 0% of the time, Pallas kernels for 7%

profile of v7, /device:TPU:1, one launch (start us, length us, event | category | flops | bytes accessed | tf_op | source)
XLA Modules:
  0.0 99.0 jit_solution(5487517831222490353)
XLA Ops:
  0.6 0.0 slice-start
  0.6 0.7 slice-done
  1.4 0.7 broadcast_in_dim.2
  2.1 7.7 %all-to-all-start = ((f32[16,32,128]{2,1,0:T(8,128)}), f32[16,32,128]{2,1,0:T(8,128)S(1)}, u32[]{:S(2)}, u32[]{:S(2)}) async-start(f32[16,32,128]{2,1,0:T(8,128)} %broadcast_in_dim.2), calls=%async_computation | async-start | bytes 524288 | tf_op jit(solution)/shard_map/all_to_all | solution.py:244
  9.8 0.0 copy-start.6
  9.8 0.0 copy-start.7
  9.9 2.4 %shard_map.103.own_ref = f32[32,4096]{1,0:T(8,128)S(1)} custom-call(f32[32,2048]{1,0:T(8,128)S(1)} %copy-done.4, s32[2,4096]{1,0:T(2,128)S(1)} %copy-done.5), custom_call_target="tpu_custom_call" | custom-call | flops 4000000000 | bytes 1048576 | tf_op jit(solution)/shard_map/pallas_call | solution.py:248
  12.2 5.1 %all-to-all-done.border_ref = f32[16,32,128]{2,1,0:T(8,128)S(1)} async-done(((f32[16,32,128]{2,1,0:T(8,128)}), f32[16,32,128]{2,1,0:T(8,128)S(1)}, u32[]{:S(2)}, u32[]{:S(2)}) %all-to-all-start) | async-done | bytes 262176 | tf_op jit(solution)/shard_map/all_to_all | solution.py:244
  17.4 0.0 copy-done.7
  17.4 5.8 %shard_map.104 = (f32[16,64,128]{2,1,0:T(8,128)}, f32[32,4096]{1,0:T(8,128)S(1)}) custom-call(f32[16,32,128]{2,1,0:T(8,128)S(1)} %all-to-all-done.border_ref, f32[32,4096]{1,0:T(8,128)S(1)} %shard_map.103.own_ref, s32[2,4096]{1,0:T(2,128)S(1)} %copy-done.5, f32[2,4096]{1,0:T(2,128)S(1)} %copy-done.6, f32[2,4096]{1,0:T(2,128)S(1)} %copy-done.7), custom_call_target="tpu_custom_call" | custom-call | flops 8000000000 | bytes 1048576 | tf_op jit(solution)/shard_map/pallas_call | solution.py:249
  23.2 3.6 %all-to-all-start.1 = ((f32[16,64,128]{2,1,0:T(8,128)}), f32[16,64,128]{2,1,0:T(8,128)S(1)}, u32[]{:S(2)}, u32[]{:S(2)}) async-start(f32[16,64,128]{2,1,0:T(8,128)} %get-tuple-element.12), calls=%async_computation.1 | async-start | bytes 1048576 | tf_op jit(solution)/shard_map/all_to_all | solution.py:254
  26.7 4.5 %shard_map.105.own_ref = f32[16,64,128]{2,1,0:T(8,128)S(1)} custom-call(f32[32,4096]{1,0:T(8,128)S(1)} %get-tuple-element.11.across_ref, s32[2,4096]{1,0:T(2,128)S(1)} %copy-done.5, f32[2,4096]{1,0:T(2,128)S(1)} %copy-done.6, f32[2,4096]{1,0:T(2,128)S(1)} %copy-done.7), custom_call_target="tpu_custom_call" | custom-call | flops 6000000000 | bytes 1048576 | tf_op jit(solution)/shard_map/pallas_call | solution.py:253
  31.3 0.0 copy-start
  31.3 0.0 copy-start.1
  31.3 4.9 %all-to-all-done.1.incoming_ref = f32[16,64,128]{2,1,0:T(8,128)S(1)} async-done(((f32[16,64,128]{2,1,0:T(8,128)}), f32[16,64,128]{2,1,0:T(8,128)S(1)}, u32[]{:S(2)}, u32[]{:S(2)}) %all-to-all-start.1) | async-done | bytes 524320 | tf_op jit(solution)/shard_map/all_to_all | solution.py:254
  36.2 0.1 shard_map.106
  36.3 28.6 %all_to_all.31 = f32[16,64,128]{2,1,0:T(8,128)S(1)} all-to-all(f32[16,64,128]{2,1,0:T(8,128)S(1)} %shard_map.106), channel_id=1, replica_groups=mesh['dom'=16,'freq'=16] {'freq'}, dimensions={0} | all-to-all | bytes 1048576 | tf_op jit(solution)/shard_map/all_to_all | solution.py:262
  64.9 0.0 copy-done
  64.9 0.7 shard_map.107
  65.6 0.0 copy-start.2
  65.6 14.5 %all_to_all.32.coef_ref = f32[16,32,128]{2,1,0:T(8,128)S(1)} all-to-all(f32[16,32,128]{2,1,0:T(8,128)S(1)} %bitcast.9), channel_id=1, replica_groups=mesh['dom'=16,'freq'=16] {'freq'}, dimensions={0} | all-to-all | bytes 524288 | tf_op jit(solution)/shard_map/all_to_all | solution.py:267
  80.2 0.7 shard_map.108
  80.8 17.3 %all_to_all.33 = f32[256,1,128]{2,1,0:T(1,128)S(1)} all-to-all(f32[256,1,128]{2,1,0:T(1,128)S(1)} %bitcast.12), channel_id=1, replica_groups=mesh['dom'=16,'freq'=16] {'dom','freq'}, dimensions={0} | all-to-all | bytes 262144 | tf_op jit(solution)/shard_map/all_to_all | solution.py:271
  98.2 0.9 shard_map.109
  (9 shorter events, 0.0 us)
Async XLA Ops:
  0.6 0.7 slice-start
  2.1 7.7 %copy-start.4 = (f32[32,2048]{1,0:T(8,128)S(1)}, f32[32,2048]{1,0:T(8,128)}, u32[]{:S(2)}) copy-start(f32[32,2048]{1,0:T(8,128)} %volt_ref.1) | copy-start | bytes 786436
  2.1 7.7 %copy-start.5 = (s32[2,4096]{1,0:T(2,128)S(1)}, s32[2,4096]{1,0:T(2,128)}, u32[]{:S(2)}) copy-start(s32[2,4096]{1,0:T(2,128)} %term_ref.5) | copy-start | bytes 98308
  2.1 15.3 %all-to-all-start = ((f32[16,32,128]{2,1,0:T(8,128)}), f32[16,32,128]{2,1,0:T(8,128)S(1)}, u32[]{:S(2)}, u32[]{:S(2)}) async-start(f32[16,32,128]{2,1,0:T(8,128)} %broadcast_in_dim.2), calls=%async_computation | async-start | bytes 524288 | tf_op jit(solution)/shard_map/all_to_all | solution.py:244
  9.8 7.5 %copy-start.6 = (f32[2,4096]{1,0:T(2,128)S(1)}, f32[2,4096]{1,0:T(2,128)}, u32[]{:S(2)}) copy-start(f32[2,4096]{1,0:T(2,128)} %cur_ref.3) | copy-start | bytes 98308
  9.8 7.5 %copy-start.7 = (f32[2,4096]{1,0:T(2,128)S(1)}, f32[2,4096]{1,0:T(2,128)}, u32[]{:S(2)}) copy-start(f32[2,4096]{1,0:T(2,128)} %chg_ref.3) | copy-start | bytes 98308
  23.2 13.0 %all-to-all-start.1 = ((f32[16,64,128]{2,1,0:T(8,128)}), f32[16,64,128]{2,1,0:T(8,128)S(1)}, u32[]{:S(2)}, u32[]{:S(2)}) async-start(f32[16,64,128]{2,1,0:T(8,128)} %get-tuple-element.12), calls=%async_computation.1 | async-start | bytes 1048576 | tf_op jit(solution)/shard_map/all_to_all | solution.py:254
  31.3 33.6 %copy-start = (bf16[512,1024]{1,0:T(8,128)(2,1)S(1)}, bf16[512,1024]{1,0:T(8,128)(2,1)}, u32[]{:S(2)}) copy-start(bf16[512,1024]{1,0:T(8,128)(2,1)} %constant.5.clone.low_ref) | copy-start | bytes 3145732
  31.3 33.6 %copy-start.1 = (bf16[512,1024]{1,0:T(8,128)(2,1)S(1)}, bf16[512,1024]{1,0:T(8,128)(2,1)}, u32[]{:S(2)}) copy-start(bf16[512,1024]{1,0:T(8,128)(2,1)} %constant.4.clone.high_ref) | copy-start | bytes 3145732
  64.9 15.3 %copy-start.3 = (f32[32,2048]{1,0:T(8,128)S(1)}, f32[32,2048]{1,0:T(8,128)}, u32[]{:S(2)}) copy-start(f32[32,2048]{1,0:T(8,128)} %src_ref.1) | copy-start | bytes 786436
  65.6 14.6 %copy-start.2 = (f32[16,2,2,2048]{3,2,1,0:T(2,128)S(1)}, f32[16,2,2,2048]{3,2,1,0:T(2,128)}, u32[]{:S(2)}) copy-start(f32[16,2,2,2048]{3,2,1,0:T(2,128)} %param.13) | copy-start | bytes 1572868
